TPU v7x, 32 devices: a whole 2x2x4 slice. The times are simulated.
32 devices in a mesh: ctx: 16 (over z, y, core), dp: 2 (over x).
Axes of the slice: x: 2, y: 2, z: 4, core: 2. Of those that a mesh axis runs over, the one named last changes fastest.
Arguments:
- query_rows: bfloat16 [2, 2048, 1024], P('dp', 'ctx'), may hold values from -6 to 6
- key_rows: bfloat16 [2, 2048, 1024], P('dp', 'ctx'), may hold values from -6 to 6
- value_rows: bfloat16 [2, 2048, 1024], P('dp', 'ctx'), may hold values from -6 to 6
- block_lists: int32 [2, 16, 4], P('dp'), may hold values from 0 to 15, as said below
- block_lengths: int32 [2, 16], P('dp'), may hold values from 2 to 128, as said below
- out_weight: bfloat16 [1024, 2048], replicated, may hold values from -0.125 to 0.125
- expert_input: bfloat16 [2, 2048, 2048], P('dp', 'ctx'), may hold values from -6 to 6
- layer_grad: bfloat16 [2, 2048, 2048], P('dp', 'ctx'), may hold values from -1.5 to 1.5
- route_experts: int32 [2, 2048, 6], P('dp', 'ctx'), may hold values from 0 to 15, all different within a row; in each aligned block of 128 rows (0 to 127, 128 to 255, ..., all dimensions but the last counted through in order) at most 64 rows name the same one
- route_weight: float32 [2, 2048, 6], P('dp', 'ctx'), may hold values from 0.02 to 0.4
- gate_weight: bfloat16 [16, 2048, 704], P('ctx'), may hold values from -0.125 to 0.125
- up_weight: bfloat16 [16, 2048, 704], P('ctx'), may hold values from -0.125 to 0.125
- down_weight: bfloat16 [16, 2048, 704], P('ctx'), may hold values from -0.21875 to 0.21875
Outputs:
- query_grad: bfloat16 [2, 2048, 1024], P('dp', 'ctx')
- key_grad: bfloat16 [2, 2048, 1024], P('dp', 'ctx')
- value_grad: bfloat16 [2, 2048, 1024], P('dp', 'ctx')
- gate_grad: float32 [16, 2048, 704], P('ctx', 'dp')
- up_grad: float32 [16, 2048, 704], P('ctx', 'dp')
- down_grad: float32 [16, 2048, 704], P('ctx', 'dp')
Inputs may be any that keep to these rules, and one draw needn't show every extreme that they name: `block_lists`: entry 0 of row i of a sequence's lists is i; every entry of row i lies in 0 to i. `block_lengths`: every sequence has a block of full length 128. `route_experts`: each token names 6 different experts. Among the 128 tokens of one device, no expert is named by more than 64 tokens.
All inputs are finite; a program needn't handle non-finite values.
Results may differ from a plain program's by a relative error of at most 0.012.
The roundings to bfloat16 on the way count: a program that leaves them out, or rounds other values in their place, can miss the bound.
Values may be sent and summed in bfloat16 or wider, within the bound.
A program may use at most 192 MiB of HBM per device.

v0:
```python
import math

import jax
import jax.numpy as jnp
from jax import lax
from jax.sharding import PartitionSpec as P

HEADS = 8
HD = 128
TOPK = 6
EXP_DEV = 1
BLK = 128
NSEL = 4


def route_coefficients(chosen, rweights, expert_list):
    matches = chosen[:, :, None] == expert_list[None, None, :]
    return jnp.sum(jnp.where(matches, rweights[:, :, None], 0.0), axis=1)


def slot_rows(tokens, grad_rows, coef_rows, capacity):
    present = coef_rows > 0.0
    rank_rows = jnp.cumsum(present.astype(jnp.int32), axis=0) - 1
    slot_ids = jnp.arange(capacity, dtype=jnp.int32)
    chosen_slot = present.T[:, None, :] & (rank_rows.T[:, None, :] == slot_ids[None, :, None])
    onehot = chosen_slot.astype(jnp.bfloat16)
    picked = jnp.einsum("ecs,sd->ecd", onehot, tokens, preferred_element_type=jnp.float32).astype(
        jnp.bfloat16
    )
    picked_grad = jnp.einsum("ecs,sd->ecd", onehot, grad_rows, preferred_element_type=jnp.float32)
    slot_coef = jnp.sum(jnp.where(chosen_slot, coef_rows.T[:, None, :], 0.0), axis=2)
    scaled = (slot_coef[:, :, None] * picked_grad).astype(jnp.bfloat16)
    return (picked, scaled)


def per_device(
    query_rows,
    key_rows,
    value_rows,
    block_lists,
    block_lengths,
    out_weight,
    expert_input,
    layer_grad,
    route_experts,
    route_weight,
    gate_weight,
    up_weight,
    down_weight,
):
    ctx_count = lax.axis_size("ctx")
    my_index = lax.axis_index("ctx")
    local_rows = query_rows.shape[1]
    seq_len = local_rows * ctx_count
    block_total = seq_len // BLK
    row_width = HEADS * HD
    inv_root = 1.0 / math.sqrt(HD)
    my_start = my_index * local_rows
    queries = query_rows[0]
    out_grad = jnp.einsum(
        "sd,wd->sw", layer_grad[0], out_weight, preferred_element_type=jnp.float32
    ).astype(jnp.bfloat16)
    whole_keys, whole_values = (
        lax.all_gather(key_rows[0], "ctx", axis=0, tiled=True),
        lax.all_gather(value_rows[0], "ctx", axis=0, tiled=True),
    )
    lengths_row = block_lengths[0]
    query_blocks = local_rows // BLK
    lists_here = lax.dynamic_slice_in_dim(block_lists[0], my_index * query_blocks, query_blocks, 0)
    entry_ids = jnp.arange(NSEL, dtype=jnp.int32)
    repeated = jnp.any(
        (lists_here[:, :, None] == lists_here[:, None, :])
        & (entry_ids[None, None, :] < entry_ids[None, :, None]),
        axis=2,
    )
    key_tiles = whole_keys.reshape(block_total, BLK, HEADS, HD)[lists_here].reshape(
        query_blocks, NSEL * BLK, HEADS, HD
    )
    value_tiles = whole_values.reshape(block_total, BLK, HEADS, HD)[lists_here].reshape(
        query_blocks, NSEL * BLK, HEADS, HD
    )
    offsets = jnp.arange(BLK, dtype=jnp.int32)
    key_pos = (lists_here[:, :, None] * BLK + offsets[None, None, :]).reshape(
        query_blocks, NSEL * BLK
    )
    present = (
        (offsets[None, None, :] < lengths_row[lists_here][:, :, None])
        & jnp.logical_not(repeated)[:, :, None]
    ).reshape(query_blocks, NSEL * BLK)
    query_pos = my_start + (
        jnp.arange(query_blocks, dtype=jnp.int32)[:, None] * BLK + offsets[None, :]
    )
    allowed = present[:, None, :] & (query_pos[:, :, None] >= key_pos[:, None, :])
    query_heads = queries.reshape(query_blocks, BLK, HEADS, HD)
    grad_heads = out_grad.reshape(query_blocks, BLK, HEADS, HD)
    raw_scores = (
        jnp.einsum("bqhd,bkhd->bhqk", query_heads, key_tiles, preferred_element_type=jnp.float32)
        * inv_root
    )
    scores = jnp.where(allowed[:, None], raw_scores, -jnp.inf)
    row_max = jnp.max(scores, axis=3)
    log_total = row_max + jnp.log(jnp.sum(jnp.exp(scores - row_max[..., None]), axis=3))
    prob_full = jnp.exp(scores - log_total[..., None])
    prob_low = prob_full.astype(jnp.bfloat16)
    head_output = jnp.einsum(
        "bhqk,bkhd->bqhd", prob_low, value_tiles, preferred_element_type=jnp.float32
    )
    row_delta = jnp.sum(head_output * grad_heads.astype(jnp.float32), axis=3)
    prob_grad = jnp.einsum(
        "bqhd,bkhd->bhqk", grad_heads, value_tiles, preferred_element_type=jnp.float32
    )
    dscore = (prob_full * (prob_grad - jnp.swapaxes(row_delta, 1, 2)[..., None])).astype(
        jnp.bfloat16
    )
    query_total = jnp.einsum(
        "bhqk,bkhd->bqhd", dscore, key_tiles, preferred_element_type=jnp.float32
    )
    query_grad = (query_total * inv_root).reshape(1, local_rows, row_width).astype(jnp.bfloat16)
    key_term = (
        jnp.einsum("bhqk,bqhd->bkhd", dscore, query_heads, preferred_element_type=jnp.float32)
        * inv_root
    )
    value_term = jnp.einsum(
        "bhqk,bqhd->bkhd", prob_low, grad_heads, preferred_element_type=jnp.float32
    )
    flat_lists = lists_here.reshape(query_blocks * NSEL)
    empty_rows = jnp.zeros((block_total, BLK, row_width), jnp.float32)
    key_part = empty_rows.at[flat_lists].add(key_term.reshape(query_blocks * NSEL, BLK, row_width))
    value_part = empty_rows.at[flat_lists].add(
        value_term.reshape(query_blocks * NSEL, BLK, row_width)
    )
    key_sum, value_sum = (
        lax.psum_scatter(
            key_part.reshape(seq_len, row_width).astype(jnp.bfloat16),
            "ctx",
            scatter_dimension=0,
            tiled=True,
        ).astype(jnp.float32),
        lax.psum_scatter(
            value_part.reshape(seq_len, row_width).astype(jnp.bfloat16),
            "ctx",
            scatter_dimension=0,
            tiled=True,
        ).astype(jnp.float32),
    )
    key_grad = key_sum.reshape(1, local_rows, row_width).astype(jnp.bfloat16)
    value_grad = value_sum.reshape(1, local_rows, row_width).astype(jnp.bfloat16)
    tokens_here = expert_input[0]
    grads_here = layer_grad[0]
    expert_count = EXP_DEV * ctx_count
    capacity = min(local_rows, local_rows * TOPK * 4 // (3 * expert_count))
    all_experts = jnp.arange(expert_count, dtype=jnp.int32)
    coef_here = route_coefficients(route_experts[0], route_weight[0], all_experts)
    picked, scaled = slot_rows(tokens_here, grads_here, coef_here, capacity)
    rows_in, grads_in = (
        lax.all_to_all(picked, "ctx", split_axis=0, concat_axis=1, tiled=True),
        lax.all_to_all(scaled, "ctx", split_axis=0, concat_axis=1, tiled=True),
    )
    gate_pre = jnp.einsum("erd,edf->erf", rows_in, gate_weight, preferred_element_type=jnp.float32)
    up_pre = jnp.einsum("erd,edf->erf", rows_in, up_weight, preferred_element_type=jnp.float32)
    gate_sig = jax.nn.sigmoid(gate_pre)
    gate_act = gate_pre * gate_sig
    hidden = (gate_act * up_pre).astype(jnp.bfloat16)
    down_part = jnp.einsum("erd,erf->edf", grads_in, hidden, preferred_element_type=jnp.float32)
    hidden_grad = jnp.einsum(
        "erd,edf->erf", grads_in, down_weight, preferred_element_type=jnp.float32
    )
    gate_delta = (hidden_grad * up_pre * gate_sig * (1.0 + gate_pre * (1.0 - gate_sig))).astype(
        jnp.bfloat16
    )
    up_delta = (hidden_grad * gate_act).astype(jnp.bfloat16)
    gate_part = jnp.einsum("erd,erf->edf", rows_in, gate_delta, preferred_element_type=jnp.float32)
    up_part = jnp.einsum("erd,erf->edf", rows_in, up_delta, preferred_element_type=jnp.float32)
    gate_grad, up_grad, down_grad = (
        lax.psum_scatter(
            gate_part.astype(jnp.bfloat16), "dp", scatter_dimension=1, tiled=True
        ).astype(jnp.float32),
        lax.psum_scatter(
            up_part.astype(jnp.bfloat16), "dp", scatter_dimension=1, tiled=True
        ).astype(jnp.float32),
        lax.psum_scatter(
            down_part.astype(jnp.bfloat16), "dp", scatter_dimension=1, tiled=True
        ).astype(jnp.float32),
    )
    return (query_grad, key_grad, value_grad, gate_grad, up_grad, down_grad)


def solution(mesh):
    in_specs = (
        P("dp", "ctx", None),
        P("dp", "ctx", None),
        P("dp", "ctx", None),
        P("dp", None, None),
        P("dp", None),
        P(),
        P("dp", "ctx", None),
        P("dp", "ctx", None),
        P("dp", "ctx", None),
        P("dp", "ctx", None),
        P("ctx", None, None),
        P("ctx", None, None),
        P("ctx", None, None),
    )
    out_specs = (
        P("dp", "ctx", None),
        P("dp", "ctx", None),
        P("dp", "ctx", None),
        P("ctx", "dp", None),
        P("ctx", "dp", None),
        P("ctx", "dp", None),
    )
    return jax.shard_map(
        per_device, mesh=mesh, in_specs=in_specs, out_specs=out_specs, check_vma=False
    )
```

profile of v0, /device:TPU:0, one launch (start us, length us, event | category | flops | bytes accessed | tf_op | source)
XLA Modules:
  0.0 563.4 jit_solution(4955409960071167728)
XLA Ops:
  9.9 4.3 convolution_convert_fusion
  14.2 7.6 %all-to-all-start = ((bf16[16,64,2048]{2,1,0:T(8,128)(2,1)}), bf16[16,64,2048]{2,1,0:T(8,128)(2,1)}, u32[]{:S(2)}, u32[]{:S(2)}) async-start(bf16[16,64,2048]{2,1,0:T(8,128)(2,1)} %convolution_convert_fusion), calls=%async_computation.2 | async-start | bytes 8388608 | tf_op jit(solution)/shard_map/all_to_all | solution.py:156
  22.8 3.2 multiply_convert_fusion
  26.0 98.8 %all-to-all-done = bf16[16,64,2048]{2,1,0:T(8,128)(2,1)} async-done(((bf16[16,64,2048]{2,1,0:T(8,128)(2,1)}), bf16[16,64,2048]{2,1,0:T(8,128)(2,1)}, u32[]{:S(2)}, u32[]{:S(2)}) %all-to-all-start) | async-done | bytes 4194336 | tf_op jit(solution)/shard_map/all_to_all | solution.py:156
  124.8 19.7 %all-to-all-start.1 = ((bf16[16,64,2048]{2,1,0:T(8,128)(2,1)}), bf16[16,64,2048]{2,1,0:T(8,128)(2,1)}, u32[]{:S(2)}, u32[]{:S(2)}) async-start(bf16[16,64,2048]{2,1,0:T(8,128)(2,1)} %multiply_convert_fusion), calls=%async_computation.3 | async-start | bytes 8388608 | tf_op jit(solution)/shard_map/all_to_all | solution.py:157
  145.5 7.1 %fusion.3 = f32[1024,704]{0,1:T(8,128)} fusion(bf16[1024,2048]{1,0:T(8,128)(2,1)} %bitcast.33, bf16[1,2048,704]{1,2,0:T(8,128)(2,1)S(1)} %copy-done), kind=kOutput, calls=%fused_computation.13 | convolution fusion | flops 2952790016 | bytes 9961472 | tf_op jit(solution)/shard_map/erd,edf->erf/dot_general | solution.py:159
  152.6 7.1 %fusion.5 = f32[1024,704]{0,1:T(8,128)} fusion(bf16[1024,2048]{1,0:T(8,128)(2,1)} %bitcast.33, bf16[1,2048,704]{1,2,0:T(8,128)(2,1)S(1)} %copy-done.10), kind=kOutput, calls=%fused_computation.15 | convolution fusion | flops 2952790016 | bytes 9961472 | tf_op jit(solution)/shard_map/erd,edf->erf/dot_general | solution.py:160
  159.7 87.7 %all-to-all-done.1 = bf16[16,64,2048]{2,1,0:T(8,128)(2,1)} async-done(((bf16[16,64,2048]{2,1,0:T(8,128)(2,1)}), bf16[16,64,2048]{2,1,0:T(8,128)(2,1)}, u32[]{:S(2)}, u32[]{:S(2)}) %all-to-all-start.1) | async-done | bytes 4194336 | tf_op jit(solution)/shard_map/all_to_all | solution.py:157
  247.4 5.1 fusion.7
  254.2 7.4 %fusion = bf16[1,2048,704]{1,2,0:T(8,128)(2,1)} fusion(bf16[1024,2048]{1,0:T(8,128)(2,1)} %bitcast.33, f32[1024,704]{0,1:T(8,128)S(1)} %copy-done.12, f32[1024,704]{0,1:T(8,128)S(1)} %fusion.7, f32[1024,704]{0,1:T(8,128)S(1)} %copy-done.14), kind=kOutput, calls=%fused_computation.10 | convolution fusion | flops 2961440768 | bytes 15728640 | tf_op jit(solution)/shard_map/erd,erf->edf/dot_general | solution.py:172
  263.3 7.8 %fusion.1 = bf16[1,2048,704]{1,2,0:T(8,128)(2,1)} fusion(bf16[1024,2048]{1,0:T(8,128)(2,1)} %bitcast.33, f32[1024,704]{0,1:T(8,128)} %copy-done.15, f32[1024,704]{0,1:T(8,128)S(1)} %copy-done.13), kind=kOutput, calls=%fused_computation.11 | convolution fusion | flops 2958557184 | bytes 12845056 | tf_op jit(solution)/shard_map/erd,erf->edf/dot_general | solution.py:173
  271.5 7.8 %fusion.2 = bf16[1,2048,704]{1,2,0:T(8,128)(2,1)} fusion(bf16[1024,2048]{1,0:T(8,128)(2,1)} %bitcast.35, f32[1024,704]{0,1:T(8,128)} %fusion.5, f32[1024,704]{0,1:T(8,128)S(1)} %copy-done.13), kind=kOutput, calls=%fused_computation.12 | convolution fusion | flops 2958557184 | bytes 12845056 | tf_op jit(solution)/shard_map/erd,erf->edf/dot_general | solution.py:164
  280.4 3.8 convolution_convert_fusion.4
  285.6 5.2 copy.93
  290.8 2.9 gather_fusion
  299.2 2.9 reshape.558
  302.1 2.9 copy.73
  305.0 4.3 broadcast_in_dim.38.clone.1
  309.2 4.5 scatter_fusion.1
  313.7 6.0 %convert_element_type.128 = bf16[16,128,1024]{2,1,0:T(8,128)(2,1)} convert(f32[16,128,1024]{2,1,0:T(8,128)} %scatter_fusion.1) | non-fusion elementwise | flops 2097152 | bytes 12582912 | tf_op jit(solution)/shard_map/convert_element_type | solution.py:140
  320.3 5.2 copy.95
  325.5 4.4 gather_fusion.2
  336.3 2.5 copy.70
  340.6 4.3 broadcast_in_dim.38.clone
  344.9 3.9 scatter_fusion
  348.8 6.0 %convert_element_type.125 = bf16[16,128,1024]{2,1,0:T(8,128)(2,1)} convert(f32[16,128,1024]{2,1,0:T(8,128)} %scatter_fusion) | non-fusion elementwise | flops 2097152 | bytes 12582912 | tf_op jit(solution)/shard_map/convert_element_type | solution.py:134
  357.6 3.3 convert_element_type.137
  360.9 3.5 convert_element_type.141
  364.4 38.3 %reduce-scatter.14.cloned.1.call-done = bf16[1,1024,704]{1,2,0:T(8,128)(2,1)} async-done(((bf16[1,2048,704]{1,2,0:T(8,128)(2,1)}), bf16[1,1024,704]{1,2,0:T(8,128)(2,1)}) %reduce-scatter.14.cloned.1.call-update) | async-done | bytes 1441808 | tf_op jit(solution)/shard_map/reduce_scatter | solution.py:181
  402.7 3.3 convert_element_type.145
  406.0 74.0 %reduce-scatter.8.cloned.1.call-done = bf16[128,1024]{1,0:T(8,128)(2,1)} async-done(((bf16[2048,1024]{1,0:T(8,128)(2,1)}), bf16[128,1024]{1,0:T(8,128)(2,1)}) %reduce-scatter.8.cloned.1.call-update) | async-done | bytes 262160 | tf_op jit(solution)/shard_map/reduce_scatter | solution.py:139
  480.0 75.8 %reduce-scatter.6.cloned.1.call-done = bf16[128,1024]{1,0:T(8,128)(2,1)} async-done(((bf16[2048,1024]{1,0:T(8,128)(2,1)}), bf16[128,1024]{1,0:T(8,128)(2,1)}) %reduce-scatter.6.cloned.1.call-update) | async-done | bytes 262160 | tf_op jit(solution)/shard_map/reduce_scatter | solution.py:133
  (89 shorter events, 26.7 us)
Async XLA Ops:
  8.0 137.5 %copy-start = (bf16[1,2048,704]{1,2,0:T(8,128)(2,1)S(1)}, bf16[1,2048,704]{1,2,0:T(8,128)(2,1)}, u32[]{:S(2)}) copy-start(bf16[1,2048,704]{1,2,0:T(8,128)(2,1)} %param.23) | copy-start | bytes 8650756
  14.2 8.6 %copy-start.7 = (bf16[1,128,2048]{2,1,0:T(8,128)(2,1)S(1)}, bf16[1,128,2048]{2,1,0:T(8,128)(2,1)}, u32[]{:S(2)}) copy-start(bf16[1,128,2048]{2,1,0:T(8,128)(2,1)} %param.20) | copy-start | bytes 1572868
  14.2 110.5 %all-to-all-start = ((bf16[16,64,2048]{2,1,0:T(8,128)(2,1)}), bf16[16,64,2048]{2,1,0:T(8,128)(2,1)}, u32[]{:S(2)}, u32[]{:S(2)}) async-start(bf16[16,64,2048]{2,1,0:T(8,128)(2,1)} %convolution_convert_fusion), calls=%async_computation.2 | async-start | bytes 8388608 | tf_op jit(solution)/shard_map/all_to_all | solution.py:156
  21.8 263.8 %all-gather.5.cloned.1.call-start = ((), (), s32[]{:S(2)}) async-start(), calls=%async_computation.12 | async-start | bytes 4456448 | tf_op jit(solution)/shard_map/all_gather | solution.py:64
  124.8 122.7 %all-to-all-start.1 = ((bf16[16,64,2048]{2,1,0:T(8,128)(2,1)}), bf16[16,64,2048]{2,1,0:T(8,128)(2,1)}, u32[]{:S(2)}, u32[]{:S(2)}) async-start(bf16[16,64,2048]{2,1,0:T(8,128)(2,1)} %multiply_convert_fusion), calls=%async_computation.3 | async-start | bytes 8388608 | tf_op jit(solution)/shard_map/all_to_all | solution.py:157
  144.5 175.8 %all-gather.7.cloned.1.call-start = ((), (), s32[]{:S(2)}) async-start(), calls=%async_computation.13 | async-start | bytes 4456448 | tf_op jit(solution)/shard_map/all_gather | solution.py:65
  145.2 212.4 %reduce-scatter.10.cloned.1.call-start = ((), (), s32[]{:S(2)}) async-start(), calls=%async_computation.9 | async-start | bytes 4325376 | tf_op jit(solution)/shard_map/reduce_scatter | solution.py:175
  145.5 7.1 %copy-start.10 = (bf16[1,2048,704]{1,2,0:T(8,128)(2,1)S(1)}, bf16[1,2048,704]{1,2,0:T(8,128)(2,1)}, u32[]{:S(2)}) copy-start(bf16[1,2048,704]{1,2,0:T(8,128)(2,1)} %param.24) | copy-start | bytes 8650756
  152.6 94.9 %copy-start.11 = (bf16[1,2048,704]{1,2,0:T(8,128)(2,1)S(1)}, bf16[1,2048,704]{1,2,0:T(8,128)(2,1)}, u32[]{:S(2)}) copy-start(bf16[1,2048,704]{1,2,0:T(8,128)(2,1)} %param.25) | copy-start | bytes 8650756
  247.4 6.7 %copy-start.12 = (f32[1024,704]{0,1:T(8,128)S(1)}, f32[1024,704]{0,1:T(8,128)}, u32[]{:S(2)}) copy-start(f32[1024,704]{0,1:T(8,128)} %fusion.3) | copy-start | bytes 8650756
  247.4 6.7 %copy-start.14 = (f32[1024,704]{0,1:T(8,128)S(1)}, f32[1024,704]{0,1:T(8,128)}, u32[]{:S(2)}) copy-start(f32[1024,704]{0,1:T(8,128)} %fusion.5) | copy-start | bytes 8650756
  252.6 1.6 copy-start.15
  261.5 1.8 copy-start.13
  261.6 99.4 %reduce-scatter.12.cloned.1.call-start = ((), (), s32[]{:S(2)}) async-start(), calls=%async_computation.10 | async-start | bytes 4325376 | tf_op jit(solution)/shard_map/reduce_scatter | solution.py:178
  271.2 131.5 %reduce-scatter.14.cloned.1.call-start = ((), (), s32[]{:S(2)}) async-start(), calls=%async_computation.11 | async-start | bytes 4325376 | tf_op jit(solution)/shard_map/reduce_scatter | solution.py:181
  279.3 0.7 copy-start.9
  279.3 1.1 copy-start.8
  279.3 200.6 %reduce-scatter.8.cloned.1.call-start = ((), (), s32[]{:S(2)}) async-start(), calls=%async_computation.8 | async-start | bytes 4456448 | tf_op jit(solution)/shard_map/reduce_scatter | solution.py:139
  280.4 4.0 copy-start.2
  319.8 236.0 %reduce-scatter.6.cloned.1.call-start = ((), (), s32[]{:S(2)}) async-start(), calls=%async_computation.7 | async-start | bytes 4456448 | tf_op jit(solution)/shard_map/reduce_scatter | solution.py:133
  332.3 1.8 copy-start.3
  334.9 1.0 copy-start.4
  354.8 1.2 copy-start.5
  354.8 1.5 copy-start.6
  360.9 194.9 %copy-start.1 = (bf16[1,2048,704]{1,2,0:T(8,128)(2,1)S(1)}, bf16[1,2048,704]{1,2,0:T(8,128)(2,1)}, u32[]{:S(2)}) copy-start(bf16[1,2048,704]{1,2,0:T(8,128)(2,1)} %param.23) | copy-start | bytes 8650756
Sparse Core Ops, SparseCore 0:
  24.8 93.9 all-gather.4
  147.5 93.9 all-gather.6
Sparse Core Ops, SparseCore 1:
  261.6 55.3 reduce-scatter.9
  319.8 40.3 reduce-scatter.11
  362.3 40.4 reduce-scatter.13
  407.7 72.3 reduce-scatter.7
  484.4 71.3 reduce-scatter.5
where the time goes:
time: 564 us; the launch traced here: 563 us
  waiting for transfers between devices  376 us (67%)
  matrix products  60.6 us (11%)
  local copies, waits for them, and re-layouts  50.7 us (9%)
  other arithmetic  31.7 us (6%)
  starting transfers between devices  28.2 us (5%)
  between operations  16 us (3%)
    all_to_all x1, waiting for transfers between devices, per_device(): lax.all_to_all(picked, 'ctx', split_axis=0, concat_axis=1, tiled=True)  98.8 us
    all_to_all x1, waiting for transfers between devices, per_device(): lax.all_to_all(scaled, 'ctx', split_axis=0, concat_axis=1, tiled=True)  87.7 us
    reduce_scatter x1, waiting for transfers between devices, per_device(): lax.psum_scatter(key_part.reshape(seq_len, row_width).astype(jnp.bfloat16...  75.8 us
    reduce_scatter x1, waiting for transfers between devices, per_device(): lax.psum_scatter(value_part.reshape(seq_len, row_width).astype(jnp.bfloat...  74 us
    reduce_scatter x1, waiting for transfers between devices, per_device(): lax.psum_scatter(down_part.astype(jnp.bfloat16), 'dp', scatter_dimension=...  38.3 us
    all_to_all x1, starting transfers between devices, per_device(): lax.all_to_all(scaled, 'ctx', split_axis=0, concat_axis=1, tiled=True)  19.7 us
    unnamed x38, local copies, waits for them, and re-layouts  19.4 us
  transfers between devices with their start and end apart: 9, of which 5 were waited for; matrix products, arithmetic and copies ran while one was open for 23% of the time, Pallas kernels for 0%

commit v1 on v0

v1 whole, which is shorter than its diff:
```python
import functools
import math

import jax
import jax.numpy as jnp
from jax import lax
from jax.experimental import pallas as pl
from jax.experimental.pallas import tpu as pltpu
from jax.sharding import PartitionSpec as P

HEADS = 8
HD = 128
TOPK = 6
BLK = 128
INV_ROOT = 1.0 / math.sqrt(HD)
MESH = pl.DeviceIdType.MESH


def ring_gather_kernel(n, x_ref, g_ref, xo_ref, go_ref, ring_send, ring_recv, sib_send, sib_recv, own_sem):
    chips = n // 2
    half_chips = chips // 2
    rows = x_ref.shape[0]
    me = lax.axis_index("ctx")
    core = me % 2
    chip = me // 2
    z, y = chip // 2, chip % 2
    pos = z + y * (chips - 1 - 2 * z)

    def device_at(p):
        p = (p + 2 * chips) % chips
        hi = p // half_chips
        return 2 * (2 * p + hi * (2 * chips - 1 - 4 * p)) + core

    sibling = me + 1 - 2 * core
    nexts = (device_at(pos + 1), device_at(pos - 1))
    ins, outs = (x_ref, g_ref), (xo_ref, go_ref)

    def piece(owner, direction, hop):
        if hop < half_chips:
            return pl.ds(pl.multiple_of(owner * rows, rows), rows)
        part = rows // 2
        return pl.ds(pl.multiple_of(owner * rows + direction * part, part), part)

    def ring_copy(src, owner, a, direction, hop):
        return pltpu.make_async_remote_copy(
            src_ref=src,
            dst_ref=outs[a].at[piece(owner, direction, hop)],
            send_sem=ring_send.at[direction, hop - 1, a],
            recv_sem=ring_recv.at[direction, hop - 1, a],
            device_id={"ctx": nexts[direction]},
            device_id_type=MESH,
        )

    def sib_copy(src, dst, a, slot):
        return pltpu.make_async_remote_copy(
            src_ref=src,
            dst_ref=dst,
            send_sem=sib_send.at[slot, a],
            recv_sem=sib_recv.at[slot, a],
            device_id={"ctx": sibling},
            device_id_type=MESH,
        )

    barrier = pltpu.get_barrier_semaphore()
    for other in (nexts[0], nexts[1], sibling):
        pl.semaphore_signal(barrier, inc=1, device_id={"ctx": other}, device_id_type=MESH)
    pl.semaphore_wait(barrier, 3)

    sends = []
    sib_waits = []
    my_rows = pl.ds(pl.multiple_of(me * rows, rows), rows)
    sib_rows = pl.ds(pl.multiple_of(sibling * rows, rows), rows)
    for a in (0, 1):
        for direction in (0, 1):
            c = ring_copy(ins[a], me, a, direction, 1)
            c.start()
            sends.append(c)
    own = []
    for a in (0, 1):
        c = sib_copy(ins[a], outs[a].at[my_rows], a, 0)
        c.start()
        sends.append(c)
        sib_waits.append(sib_copy(outs[a].at[sib_rows], outs[a].at[sib_rows], a, 0))
        local = pltpu.make_async_copy(ins[a], outs[a].at[my_rows], own_sem.at[a])
        local.start()
        own.append(local)
    for hop in range(1, half_chips + 1):
        for a in (0, 1):
            for direction in (0, 1):
                step = hop if direction == 0 else -hop
                owner = device_at(pos - step)
                here = outs[a].at[piece(owner, direction, hop)]
                ring_copy(here, owner, a, direction, hop).wait_recv()
                if hop < half_chips:
                    onward = outs[a].at[piece(owner, direction, hop + 1)]
                    c = ring_copy(onward, owner, a, direction, hop + 1)
                    c.start()
                    sends.append(c)
                slot = 1 + 2 * (hop - 1) + direction
                c = sib_copy(here, here, a, slot)
                c.start()
                sends.append(c)
                other = owner + 1 - 2 * core
                there = outs[a].at[piece(other, direction, hop)]
                sib_waits.append(sib_copy(there, there, a, slot))
    for c in own:
        c.wait()
    for c in sib_waits:
        c.wait_recv()
    for c in sends:
        c.wait_send()


def ring_gather(x, g):
    n = lax.axis_size("ctx")
    hops = n // 4
    rows, width = x.shape
    out = jax.ShapeDtypeStruct((n * rows, width), x.dtype)
    return pl.pallas_call(
        functools.partial(ring_gather_kernel, n),
        out_shape=(out, out),
        in_specs=[pl.BlockSpec(memory_space=pl.ANY)] * 2,
        out_specs=(pl.BlockSpec(memory_space=pl.ANY),) * 2,
        scratch_shapes=[
            pltpu.SemaphoreType.DMA((2, hops, 2)),
            pltpu.SemaphoreType.DMA((2, hops, 2)),
            pltpu.SemaphoreType.DMA((1 + 2 * hops, 2)),
            pltpu.SemaphoreType.DMA((1 + 2 * hops, 2)),
            pltpu.SemaphoreType.DMA((2,)),
        ],
        compiler_params=pltpu.CompilerParams(collective_id=0, has_side_effects=True),
        cost_estimate=pl.CostEstimate(
            flops=0, bytes_accessed=4 * n * rows * width * 2, transcendentals=0
        ),
        name="ring_gather",
    )(x, g)


def dot_rows(a, b):
    return lax.dot_general(a, b, (((1,), (1,)), ((), ())), preferred_element_type=jnp.float32)


def query_kernel(q_ref, k_ref, v_ref, g_ref, open_ref, off_ref, qg_ref, lt_ref, rd_ref):
    keys = k_ref.shape[0]
    rows = q_ref.shape[0]
    key_pos = lax.broadcasted_iota(jnp.int32, (keys, rows), 0)
    query_pos = lax.broadcasted_iota(jnp.int32, (keys, rows), 1) + off_ref[0]
    allowed = (open_ref[...] > 0) & (key_pos <= query_pos)
    k, v, q, g = k_ref[...], v_ref[...], q_ref[...], g_ref[...]
    scores = jnp.where(allowed, dot_rows(k, q) * INV_ROOT, -jnp.inf)
    row_max = jnp.max(scores, axis=0, keepdims=True)
    log_total = row_max + jnp.log(jnp.sum(jnp.exp(scores - row_max), axis=0, keepdims=True))
    prob = jnp.exp(scores - log_total)
    prob_low = prob.astype(jnp.bfloat16)
    prob_grad = dot_rows(v, g)
    row_delta = jnp.sum(prob_low.astype(jnp.float32) * prob_grad, axis=0, keepdims=True)
    dscore = (prob * (prob_grad - row_delta)).astype(jnp.bfloat16)
    total = lax.dot_general(
        dscore, k, (((0,), (0,)), ((), ())), preferred_element_type=jnp.float32
    )
    qg_ref[...] = (total * INV_ROOT).astype(jnp.bfloat16)
    lt_ref[0] = log_total
    rd_ref[0] = row_delta


def query_side(q, k_all, v_all, g, key_open, offset):
    rows = q.shape[0]
    keys = k_all.shape[0]
    heads = q.shape[1] // HD
    return pl.pallas_call(
        query_kernel,
        grid=(heads,),
        out_shape=(
            jax.ShapeDtypeStruct(q.shape, jnp.bfloat16),
            jax.ShapeDtypeStruct((heads, 1, rows), jnp.float32),
            jax.ShapeDtypeStruct((heads, 1, rows), jnp.float32),
        ),
        in_specs=[
            pl.BlockSpec((rows, HD), lambda h: (0, h)),
            pl.BlockSpec((keys, HD), lambda h: (0, h)),
            pl.BlockSpec((keys, HD), lambda h: (0, h)),
            pl.BlockSpec((rows, HD), lambda h: (0, h)),
            pl.BlockSpec((keys, 1), lambda h: (0, 0)),
            pl.BlockSpec(memory_space=pltpu.SMEM),
        ],
        out_specs=(
            pl.BlockSpec((rows, HD), lambda h: (0, h)),
            pl.BlockSpec((1, 1, rows), lambda h: (h, 0, 0)),
            pl.BlockSpec((1, 1, rows), lambda h: (h, 0, 0)),
        ),
        compiler_params=pltpu.CompilerParams(vmem_limit_bytes=40 * 1024 * 1024),
        cost_estimate=pl.CostEstimate(
            flops=6 * heads * rows * keys * HD,
            bytes_accessed=4 * heads * keys * HD,
            transcendentals=2 * heads * rows * keys,
        ),
        name="query_side",
    )(q, k_all, v_all, g, key_open, offset)


def key_kernel(k_ref, v_ref, q_ref, g_ref, lt_ref, rd_ref, listed_ref, open_ref, off_ref, kg_ref, vg_ref):
    keys = k_ref.shape[0]
    queries = q_ref.shape[0]
    key_pos = lax.broadcasted_iota(jnp.int32, (keys, queries), 0) + off_ref[0]
    query_pos = lax.broadcasted_iota(jnp.int32, (keys, queries), 1)
    allowed = (listed_ref[...] > 0) & (open_ref[...] > 0) & (key_pos <= query_pos)
    k, v, q, g = k_ref[...], v_ref[...], q_ref[...], g_ref[...]
    scores = jnp.where(allowed, dot_rows(k, q) * INV_ROOT, -jnp.inf)
    prob = jnp.exp(scores - lt_ref[0])
    prob_low = prob.astype(jnp.bfloat16)
    prob_grad = dot_rows(v, g)
    dscore = (prob * (prob_grad - rd_ref[0])).astype(jnp.bfloat16)
    vg_ref[...] = jnp.dot(prob_low, g, preferred_element_type=jnp.float32).astype(jnp.bfloat16)
    kg_ref[...] = (jnp.dot(dscore, q, preferred_element_type=jnp.float32) * INV_ROOT).astype(
        jnp.bfloat16
    )


def key_side(k, v, q_all, g_all, log_total, row_delta, listed, key_open, offset):
    keys = k.shape[0]
    queries = q_all.shape[0]
    heads = k.shape[1] // HD
    small = pl.BlockSpec((keys, HD), lambda h: (0, h))
    large = pl.BlockSpec((queries, HD), lambda h: (0, h))
    stat = pl.BlockSpec((1, 1, queries), lambda h: (h, 0, 0))
    out = jax.ShapeDtypeStruct(k.shape, jnp.bfloat16)
    return pl.pallas_call(
        key_kernel,
        grid=(heads,),
        out_shape=(out, out),
        in_specs=[
            small,
            small,
            large,
            large,
            stat,
            stat,
            pl.BlockSpec((1, queries), lambda h: (0, 0)),
            pl.BlockSpec((keys, 1), lambda h: (0, 0)),
            pl.BlockSpec(memory_space=pltpu.SMEM),
        ],
        out_specs=(small, small),
        compiler_params=pltpu.CompilerParams(vmem_limit_bytes=40 * 1024 * 1024),
        cost_estimate=pl.CostEstimate(
            flops=8 * heads * keys * queries * HD,
            bytes_accessed=4 * heads * queries * HD,
            transcendentals=heads * keys * queries,
        ),
        name="key_side",
    )(k, v, q_all, g_all, log_total, row_delta, listed, key_open, offset)


def per_device(
    query_rows,
    key_rows,
    value_rows,
    block_lists,
    block_lengths,
    out_weight,
    expert_input,
    layer_grad,
    route_experts,
    route_weight,
    gate_weight,
    up_weight,
    down_weight,
):
    n = lax.axis_size("ctx")
    dp = lax.axis_size("dp")
    me = lax.axis_index("ctx")
    my_dp = lax.axis_index("dp")
    rows = query_rows.shape[1]
    seq_len = rows * n
    blocks = seq_len // BLK
    width = expert_input.shape[2]

    experts = jnp.arange(n, dtype=jnp.int32)
    matches = route_experts[0].T[None, :, :] == experts[:, None, None]
    coef_here = jnp.sum(jnp.where(matches, route_weight[0].T[None, :, :], 0.0), axis=1)
    coef_all = lax.all_gather(coef_here, "ctx", axis=0)
    coef = lax.dynamic_index_in_dim(coef_all, me, axis=1, keepdims=False)

    k_all = lax.all_gather(key_rows[0], "ctx", axis=0, tiled=True)
    v_all = lax.all_gather(value_rows[0], "ctx", axis=0, tiled=True)
    q_all = lax.all_gather(query_rows[0], "ctx", axis=0, tiled=True)
    x_all, g_all = ring_gather(expert_input[0], layer_grad[0])

    capacity = min(rows, rows * TOPK * 4 // (3 * n))
    present = coef > 0.0
    rank = jnp.cumsum(present.astype(jnp.int32), axis=1) - 1
    slots = jnp.arange(capacity, dtype=jnp.int32)
    chosen = present[:, None, :] & (rank[:, None, :] == slots[None, :, None])
    onehot = chosen.astype(jnp.bfloat16)
    slot_coef = jnp.sum(jnp.where(chosen, coef[:, None, :], 0.0), axis=2)
    picked = jnp.einsum(
        "ics,isd->icd", onehot, x_all.reshape(n, rows, width), preferred_element_type=jnp.float32
    ).astype(jnp.bfloat16)
    picked_grad = jnp.einsum(
        "ics,isd->icd", onehot, g_all.reshape(n, rows, width), preferred_element_type=jnp.float32
    )
    scaled = (slot_coef[:, :, None] * picked_grad).astype(jnp.bfloat16)
    tokens = picked.reshape(n * capacity, width)
    grads = scaled.reshape(n * capacity, width)

    gate_pre = jnp.dot(tokens, gate_weight[0], preferred_element_type=jnp.float32)
    up_pre = jnp.dot(tokens, up_weight[0], preferred_element_type=jnp.float32)
    hidden_grad = jnp.dot(grads, down_weight[0], preferred_element_type=jnp.float32)
    gate_sig = jax.nn.sigmoid(gate_pre)
    gate_act = gate_pre * gate_sig
    hidden = (gate_act * up_pre).astype(jnp.bfloat16)
    gate_delta = (hidden_grad * up_pre * gate_sig * (1.0 + gate_pre * (1.0 - gate_sig))).astype(
        jnp.bfloat16
    )
    up_delta = (hidden_grad * gate_act).astype(jnp.bfloat16)

    def partial(a, b):
        return lax.dot_general(
            a, b, (((0,), (0,)), ((), ())), preferred_element_type=jnp.float32
        ).astype(jnp.bfloat16)

    pairs = ((grads, hidden), (tokens, gate_delta), (tokens, up_delta))
    if dp == 2:
        half = width // 2
        swap = [(0, 1), (1, 0)]
        arrived = [
            lax.ppermute(
                partial(lax.dynamic_slice_in_dim(a, (1 - my_dp) * half, half, 1), b), "dp", swap
            )
            for a, b in pairs
        ]
        sums = [
            partial(lax.dynamic_slice_in_dim(a, my_dp * half, half, 1), b).astype(jnp.float32)
            + r.astype(jnp.float32)
            for (a, b), r in zip(pairs, arrived)
        ]
    else:
        sums = [
            lax.psum_scatter(partial(a, b), "dp", scatter_dimension=0, tiled=True).astype(
                jnp.float32
            )
            for a, b in pairs
        ]
    down_grad, gate_grad, up_grad = (s[None] for s in sums)

    out_all = lax.dot_general(
        g_all, out_weight, (((1,), (1,)), ((), ())), preferred_element_type=jnp.float32
    ).astype(jnp.bfloat16)
    out_here = lax.dynamic_slice_in_dim(out_all, me * rows, rows, 0)
    lists = block_lists[0]
    lengths = block_lengths[0]
    block_ids = jnp.arange(blocks, dtype=jnp.int32)
    offsets = jnp.arange(BLK, dtype=jnp.int32)
    valid = offsets[None, :] < lengths[:, None]
    my_list = lax.dynamic_index_in_dim(lists, me, 0, keepdims=False)
    my_blocks = jnp.any(my_list[None, :] == block_ids[:, None], axis=1)
    open_all = (my_blocks[:, None] & valid).astype(jnp.int32).reshape(seq_len, 1)
    offset = jnp.reshape(me * rows, (1,)).astype(jnp.int32)
    query_grad, log_total, row_delta = query_side(
        query_rows[0], k_all, v_all, out_here, open_all, offset
    )
    stats = jnp.stack([log_total[:, 0], row_delta[:, 0]])
    stats_all = lax.all_gather(stats, "ctx", axis=2, tiled=True)
    lists_me = jnp.any(lists == me, axis=1)
    listed = jnp.broadcast_to(lists_me[:, None], (blocks, BLK)).astype(jnp.int32)
    my_open = lax.dynamic_index_in_dim(valid, me, 0, keepdims=False).astype(jnp.int32)
    key_grad, value_grad = key_side(
        key_rows[0],
        value_rows[0],
        q_all,
        out_all,
        stats_all[0][:, None, :],
        stats_all[1][:, None, :],
        listed.reshape(1, seq_len),
        my_open.reshape(BLK, 1),
        offset,
    )
    return (query_grad[None], key_grad[None], value_grad[None], gate_grad, up_grad, down_grad)


def solution(mesh):
    in_specs = (
        P("dp", "ctx", None),
        P("dp", "ctx", None),
        P("dp", "ctx", None),
        P("dp", None, None),
        P("dp", None),
        P(),
        P("dp", "ctx", None),
        P("dp", "ctx", None),
        P("dp", "ctx", None),
        P("dp", "ctx", None),
        P("ctx", None, None),
        P("ctx", None, None),
        P("ctx", None, None),
    )
    out_specs = (
        P("dp", "ctx", None),
        P("dp", "ctx", None),
        P("dp", "ctx", None),
        P("ctx", "dp", None),
        P("ctx", "dp", None),
        P("ctx", "dp", None),
    )
    return jax.shard_map(
        per_device, mesh=mesh, in_specs=in_specs, out_specs=out_specs, check_vma=False
    )
```

time: 564 us -> 353 us (0.63)
  waiting for transfers between devices: 376 us -> 66.5 us
  Pallas kernels: 0 us -> 154 us
  blocking collectives: 0 us -> 41.1 us
  local copies, waits for them, and re-layouts: 50.7 us -> 15.6 us
  other arithmetic: 31.7 us -> 0.77 us
  starting transfers between devices: 28.2 us -> 3.58 us
    reduce_scatter x5 -> x0, waiting for transfers between devices: 188 us -> none  [the longest x1 75.8 us: per_device(): lax.psum_scatter(key_part.reshape(seq_len, row_width).astype(jnp.bfloat16...]
    all_to_all x2 -> x0, waiting for transfers between devices: 187 us -> none  [the longest x1 98.8 us: per_device(): lax.all_to_all(picked, 'ctx', split_axis=0, concat_axis=1, tiled=True)]
    pallas_call x0 -> x3, Pallas kernels: none -> 154 us  [the longest x1 126 us: ring_gather(): pl.pallas_call(functools.partial(ring_gather_kernel, n), out_shape=(out,...]
    ppermute x0 -> x3, waiting for transfers between devices: none -> 64.4 us  [per_device(): lax.ppermute(partial(lax.dynamic_slice_in_dim(a, (1 - my_dp) * half, half...]
    all_gather x0 -> x2, blocking collectives: none -> 41.1 us  [the longest x1 23.7 us: per_device(): coef_all = lax.all_gather(coef_here, 'ctx', axis=0)]
    all_to_all x2 -> x0, starting transfers between devices: 27.3 us -> none  [the longest x1 19.7 us: per_device(): lax.all_to_all(scaled, 'ctx', split_axis=0, concat_axis=1, tiled=True)]
    convert_element_type x6 -> x2, other arithmetic: 22.1 us -> 0.02 us  [the longest x1 0.01 us: per_device(): lax.dynamic_index_in_dim(valid, me, 0, keepdims=False).astype(jnp.int32)]
    broadcast_in_dim x2 -> x1, local copies, waits for them, and re-layouts: 8.58 us -> 0.07 us  [per_device(): jnp.broadcast_to(lists_me[:, None], (blocks, BLK)).astype(jnp.int32)]
  transfers between devices with their start and end apart: 9 -> 6, of which waited for: 5 -> 3; matrix products, arithmetic and copies ran while one was open for 23% -> 18% of each run, Pallas kernels for 0% -> 41%
where the time goes in v1:
time: 353 us
  Pallas kernels  154 us (44%)
  waiting for transfers between devices  66.5 us (19%)
  matrix products  57.2 us (16%)
  blocking collectives  41.1 us (12%)
  local copies, waits for them, and re-layouts  15.6 us (4%)
  between operations  14 us (4%)
  starting transfers between devices  3.58 us (1%)
    pallas_call x1, Pallas kernels, ring_gather(): pl.pallas_call(functools.partial(ring_gather_kernel, n), out_shape=(out,...  126 us
    ppermute x3, waiting for transfers between devices, per_device(): lax.ppermute(partial(lax.dynamic_slice_in_dim(a, (1 - my_dp) * half, half...  64.4 us
    all_gather x1, blocking collectives, per_device(): coef_all = lax.all_gather(coef_here, 'ctx', axis=0)  23.7 us
    dot_general x6, matrix products, partial(): lax.dot_general(a, b, (((0,), (0,)), ((), ())), preferred_element_type=jn...  23.2 us
    all_gather x1, blocking collectives, per_device(): stats_all = lax.all_gather(stats, 'ctx', axis=2, tiled=True)  17.5 us
    pallas_call x1, Pallas kernels, query_side(): pl.pallas_call(query_kernel, grid=(heads,), out_shape=(jax.ShapeDtypeStru...  16.7 us
    unnamed x60, local copies, waits for them, and re-layouts  13.2 us
    pallas_call x1, Pallas kernels, key_side(): pl.pallas_call(key_kernel, grid=(heads,), out_shape=(out, out), in_specs=...  10.9 us
  transfers between devices with their start and end apart: 6, of which 3 were waited for; matrix products, arithmetic and copies ran while one was open for 18% of the time, Pallas kernels for 41%

profile of v1, /device:TPU:0, one launch (start us, length us, event | category | flops | bytes accessed | tf_op | source)
XLA Modules:
  0.0 352.6 jit_solution(7539087088810089244)
XLA Ops:
  8.0 0.7 all-gather.10.cloned.1.call-update
  10.8 23.7 %all-gather.3 = f32[256,128]{1,0:T(8,128)S(1)} all-gather(f32[16,128]{1,0:T(8,128)S(1)} %select_reduce_fusion.1), channel_id=5, replica_groups=mesh['ctx'=16,'dp'=2] {'ctx'}, dimensions={0}, use_global_device_ids=true | all-gather | bytes 139264 | tf_op jit(solution)/shard_map/all_gather | solution.py:280
  34.8 126.2 %ring_gather.1 = (bf16[2048,2048]{1,0:T(8,128)(2,1)}, bf16[2048,2048]{1,0:T(8,128)(2,1)}) custom-call(bf16[128,2048]{1,0:T(8,128)(2,1)} %bitcast.96, bf16[128,2048]{1,0:T(8,128)(2,1)} %bitcast.97), custom_call_target="tpu_custom_call" | custom-call | bytes 33554432 | tf_op jit(solution)/shard_map/ring_gather/pallas_call | solution.py:119
  161.3 5.0 %convolution_convert_fusion.1 = bf16[16,64,2048]{2,1,0:T(8,128)(2,1)S(1)} fusion(bf16[16,128,2048]{2,1,0:T(8,128)(2,1)} %bitcast.86, s32[16,128]{1,0:T(8,128)S(1)} %broadcast_add_fusion, pred[16,128]{1,0:T(8,128)(4,1)S(1)} %get-tuple-element.21), kind=kOutput, calls=%fused_computation.2 | convolution fusion | flops 539230208 | bytes 12593152 | tf_op jit(solution)/shard_map/ics,isd->icd/dot_general | solution.py:295
  166.3 1.1 slice-done.1
  167.5 1.3 multiply_convert_fusion
  168.8 0.9 copy-done.18
  169.6 4.8 %fusion.4 = f32[1024,704]{0,1:T(8,128)} fusion(bf16[1024,2048]{1,0:T(8,128)(2,1)S(1)} %bitcast.87, bf16[1,2048,704]{1,2,0:T(8,128)(2,1)S(1)} %copy-done.18), kind=kOutput, calls=%fused_computation.7 | convolution fusion | flops 2952790016 | bytes 9961472 | tf_op jit(solution)/shard_map/dot_general | solution.py:307
  174.4 4.8 %fusion = f32[1024,704]{0,1:T(8,128)} fusion(bf16[1024,2048]{1,0:T(8,128)(2,1)S(1)} %bitcast.90, bf16[1,2048,704]{1,2,0:T(8,128)(2,1)S(1)} %copy-done.19), kind=kOutput, calls=%fused_computation.3 | convolution fusion | flops 2952790016 | bytes 9961472 | tf_op jit(solution)/shard_map/dot_general | solution.py:305
  179.1 7.6 %multiply_convert_fusion.1 = (bf16[1024,704]{0,1:T(8,128)(2,1)S(1)}, bf16[1024,704]{0,1:T(8,128)(2,1)S(1)}, bf16[1024,704]{0,1:T(8,128)(2,1)S(1)}) fusion(f32[1024,704]{0,1:T(8,128)} %fusion, f32[1024,704]{0,1:T(8,128)} %fusion.4, bf16[1024,2048]{1,0:T(8,128)(2,1)} %bitcast.91, bf16[1,2048,704]{1,2,0:T(8,128)(2,1)S(1)} %copy-done), kind=kOutput, calls=%fused_computation.10 | convolution fusion | flops 2963603456 | bytes 17170432 | tf_op jit(solution)/shard_map/dot_general | solution.py:306
  186.8 2.8 fusion.34
  189.6 1.4 collective-permute-start.2
  191.0 2.8 fusion.25
  193.8 1.4 collective-permute-start.1
  195.2 2.8 fusion.28
  198.6 10.5 %convolution_convert_fusion.g_ref = bf16[2048,1024]{1,0:T(8,128)(2,1)} fusion(bf16[2048,2048]{1,0:T(8,128)(2,1)S(1)} %bitcast.85, bf16[1024,2048]{1,0:T(8,128)(2,1)S(1)} %copy-done.17), kind=kOutput, calls=%fused_computation.1 | convolution fusion | flops 8592031744 | bytes 16777216 | tf_op jit(solution)/shard_map/dot_general | solution.py:345
  210.0 1.0 constant_dynamic-slice_fusion.2.g_ref
  211.0 13.3 %collective-permute-done.2 = bf16[1024,704]{0,1:T(8,128)(2,1)} collective-permute-done((bf16[1024,704]{0,1:T(8,128)(2,1)}, bf16[1024,704]{0,1:T(8,128)(2,1)}, u32[]{:S(2)}, u32[]{:S(2)}) %collective-permute-start.2) | collective-permute-done | bytes 1441824 | tf_op jit(solution)/shard_map/ppermute | solution.py:326
  224.3 5.7 %add_bitcast_fusion = f32[1,1024,704]{1,2,0:T(8,128)} fusion(bf16[1024,704]{0,1:T(8,128)(2,1)} %collective-permute-done.2, bf16[1024,704]{0,1:T(8,128)(2,1)} %copy-done.24, bf16[1024,2048]{1,0:T(8,128)(2,1)} %bitcast.88, s32[]{:T(128)S(6)} %select_n.32), kind=kOutput, calls=%fused_computation.9 | convolution fusion | flops 1479278592 | bytes 7864324 | tf_op jit(solution)/shard_map/dot_general | solution.py:317
  229.9 25.2 %collective-permute-done.1 = bf16[1024,704]{0,1:T(8,128)(2,1)} collective-permute-done((bf16[1024,704]{0,1:T(8,128)(2,1)}, bf16[1024,704]{0,1:T(8,128)(2,1)}, u32[]{:S(2)}, u32[]{:S(2)}) %collective-permute-start.1) | collective-permute-done | bytes 1441824 | tf_op jit(solution)/shard_map/ppermute | solution.py:326
  255.2 4.7 %add_bitcast_fusion.1 = f32[1,1024,704]{1,2,0:T(8,128)} fusion(bf16[1024,704]{0,1:T(8,128)(2,1)} %collective-permute-done.1, bf16[1024,704]{0,1:T(8,128)(2,1)S(1)} %copy-done.23, bf16[1024,2048]{1,0:T(8,128)(2,1)S(1)} %bitcast.94, s32[]{:T(128)S(6)} %select_n.32), kind=kOutput, calls=%fused_computation.11 | convolution fusion | flops 1479278592 | bytes 7864324 | tf_op jit(solution)/shard_map/dot_general | solution.py:317
  259.8 25.9 %collective-permute-done = bf16[1024,704]{0,1:T(8,128)(2,1)} collective-permute-done((bf16[1024,704]{0,1:T(8,128)(2,1)}, bf16[1024,704]{0,1:T(8,128)(2,1)}, u32[]{:S(2)}, u32[]{:S(2)}) %collective-permute-start) | collective-permute-done | bytes 1441824 | tf_op jit(solution)/shard_map/ppermute | solution.py:326
  285.8 4.6 %add_bitcast_fusion.2 = f32[1,1024,704]{1,2,0:T(8,128)} fusion(bf16[1024,704]{0,1:T(8,128)(2,1)} %collective-permute-done, bf16[1024,704]{0,1:T(8,128)(2,1)S(1)} %copy-done.21, bf16[1024,2048]{1,0:T(8,128)(2,1)S(1)} %bitcast.95, s32[]{:T(128)S(6)} %select_n.32), kind=kOutput, calls=%fused_computation.13 | convolution fusion | flops 1479278592 | bytes 7864324 | tf_op jit(solution)/shard_map/dot_general | solution.py:317
  290.4 2.2 copy-done.3
  292.6 2.2 copy-done.4
  294.8 16.7 %query_side.1 = (bf16[128,1024]{1,0:T(8,128)(2,1)}, f32[8,1,128]{2,1,0:T(1,128)S(1)}, f32[8,1,128]{2,1,0:T(1,128)S(1)}) custom-call(bf16[128,1024]{1,0:T(8,128)(2,1)S(1)} %bitcast.75, bf16[2048,1024]{1,0:T(8,128)(2,1)S(1)} %bitcast.72, bf16[2048,1024]{1,0:T(8,128)(2,1)S(1)} %bitcast.73, bf16[128,1024]{1,0:T(8,128)(2,1)S(1)} %constant_dynamic-slice_fusion.2.g_ref, ...), custom_call_target="tpu_custom_call" | custom-call | flops 1610612736 | bytes 8388608 | tf_op jit(solution)/shard_map/query_side/pallas_call | solution.py:170
  311.5 17.5 %all_gather.21 = f32[2,8,2048]{2,0,1:T(2,128)S(1)} all-gather(f32[2,8,128]{2,0,1:T(2,128)S(1)} %pad_maximum_fusion), channel_id=1, replica_groups=mesh['ctx'=16,'dp'=2] {'ctx'}, dimensions={2}, use_global_device_ids=true | all-gather | bytes 139264 | tf_op jit(solution)/shard_map/all_gather | solution.py:362
  329.0 0.7 slice_bitcast_fusion
  329.8 2.3 copy-done.2
  332.2 2.2 copy-done.5
  334.4 0.8 copy-done.9
  335.2 10.9 %key_side.1 = (bf16[128,1024]{1,0:T(8,128)(2,1)}, bf16[128,1024]{1,0:T(8,128)(2,1)}) custom-call(bf16[128,1024]{1,0:T(8,128)(2,1)S(1)} %bitcast.76, bf16[128,1024]{1,0:T(8,128)(2,1)S(1)} %bitcast.77, bf16[2048,1024]{1,0:T(8,128)(2,1)S(1)} %bitcast.74, bf16[2048,1024]{1,0:T(8,128)(2,1)S(1)} %copy-done.2, f32[8,1,2048]{2,1,0:T(1,128)S(1)} %copy-done.9, ...), custom_call_target="tpu_custom_call" | custom-call | flops 2147483648 | bytes 8388608 | tf_op jit(solution)/shard_map/key_side/pallas_call | solution.py:227
  (80 shorter events, 5.1 us)
Async XLA Ops:
  7.2 172.0 %copy-start = (bf16[1,2048,704]{1,2,0:T(8,128)(2,1)S(1)}, bf16[1,2048,704]{1,2,0:T(8,128)(2,1)}, u32[]{:S(2)}) copy-start(bf16[1,2048,704]{1,2,0:T(8,128)(2,1)} %param.24) | copy-start | bytes 8650756
  7.2 283.2 %all-gather.8.cloned.1.call-start = ((), (), s32[]{:S(2)}) async-start(), calls=%async_computation | async-start | bytes 4456448 | tf_op jit(solution)/shard_map/all_gather | solution.py:283
  7.9 282.5 %all-gather.10.cloned.1.call-start = ((), (), s32[]{:S(2)}) async-start(), calls=%async_computation.1 | async-start | bytes 4456448 | tf_op jit(solution)/shard_map/all_gather | solution.py:284
  8.7 321.1 %all-gather.12.cloned.1.call-start = ((), (), s32[]{:S(2)}) async-start(), calls=%async_computation.2 | async-start | bytes 4456448 | tf_op jit(solution)/shard_map/all_gather | solution.py:285
  161.2 5.1 %slice-start = ((s8[8388608]{0:T(1024)(128)(4,1)}), s8[4194304]{0:T(1024)(128)(4,1)S(1)}, s32[]{:S(2)}) async-start(s8[8388608]{0:T(1024)(128)(4,1)} %bitcast.81), calls=%async_computation.3 | async-start | bytes 8388608
  161.3 6.2 %slice-start.1 = ((s8[8388608]{0:T(1024)(128)(4,1)}), s8[4194304]{0:T(1024)(128)(4,1)S(1)}, s32[]{:S(2)}) async-start(s8[8388608]{0:T(1024)(128)(4,1)} %bitcast.81), calls=%async_computation.4 | async-start | bytes 8388608
  166.3 8.1 %copy-start.12 = (bf16[16,64,2048]{2,1,0:T(8,128)(2,1)}, bf16[16,64,2048]{2,1,0:T(8,128)(2,1)S(1)}, u32[]{:S(2)}) copy-start(bf16[16,64,2048]{2,1,0:T(8,128)(2,1)S(1)} %convolution_convert_fusion.1) | copy-start | bytes 12582916
  168.7 5.6 %copy-start.10 = (bf16[16,64,2048]{2,1,0:T(8,128)(2,1)}, bf16[16,64,2048]{2,1,0:T(8,128)(2,1)S(1)}, u32[]{:S(2)}) copy-start(bf16[16,64,2048]{2,1,0:T(8,128)(2,1)S(1)} %multiply_convert_fusion) | copy-start | bytes 12582916
  169.6 4.8 %copy-start.19 = (bf16[1,2048,704]{1,2,0:T(8,128)(2,1)S(1)}, bf16[1,2048,704]{1,2,0:T(8,128)(2,1)}, u32[]{:S(2)}) copy-start(bf16[1,2048,704]{1,2,0:T(8,128)(2,1)} %param.23) | copy-start | bytes 8650756
  179.1 7.7 %copy-start.11 = (bf16[16,64,2048]{2,1,0:T(8,128)(2,1)S(1)}, bf16[16,64,2048]{2,1,0:T(8,128)(2,1)}, u32[]{:S(2)}) copy-start(bf16[16,64,2048]{2,1,0:T(8,128)(2,1)} %copy-done.10) | copy-start | bytes 12582916
  186.8 2.8 copy-start.24
  186.8 4.3 %copy-start.22 = (bf16[1024,704]{0,1:T(8,128)(2,1)}, bf16[1024,704]{0,1:T(8,128)(2,1)S(1)}, u32[]{:S(2)}) copy-start(bf16[1024,704]{0,1:T(8,128)(2,1)S(1)} %get-tuple-element.26) | copy-start | bytes 4325380
  186.8 8.5 %copy-start.20 = (bf16[1024,704]{0,1:T(8,128)(2,1)}, bf16[1024,704]{0,1:T(8,128)(2,1)S(1)}, u32[]{:S(2)}) copy-start(bf16[1024,704]{0,1:T(8,128)(2,1)S(1)} %get-tuple-element.25) | copy-start | bytes 4325380
  186.8 4.2 %copy-start.13 = (bf16[16,64,2048]{2,1,0:T(8,128)(2,1)S(1)}, bf16[16,64,2048]{2,1,0:T(8,128)(2,1)}, u32[]{:S(2)}) copy-start(bf16[16,64,2048]{2,1,0:T(8,128)(2,1)} %copy-done.12) | copy-start | bytes 12582916
  189.6 34.7 %collective-permute-start.2 = (bf16[1024,704]{0,1:T(8,128)(2,1)}, bf16[1024,704]{0,1:T(8,128)(2,1)}, u32[]{:S(2)}, u32[]{:S(2)}) collective-permute-start(bf16[1024,704]{0,1:T(8,128)(2,1)} %fusion.34), channel_id=1, source_target_pairs={{0,1},{1,0},{2,3},{3,2},{4,5},{5,4},{6,7},{7,6},{8,9},{9,8},{10,11... | collective-permute-start | bytes 4325384 | tf_op jit(solution)/shard_map/ppermute | solution.py:326
  191.0 7.6 %slice-start.2 = ((s8[8388608]{0:T(1024)(128)(4,1)}), s8[4194304]{0:T(1024)(128)(4,1)S(1)}, s32[]{:S(2)}) async-start(s8[8388608]{0:T(1024)(128)(4,1)} %bitcast.84), calls=%async_computation.5 | async-start | bytes 8388608
  193.8 4.8 %slice-start.3 = ((s8[8388608]{0:T(1024)(128)(4,1)}), s8[4194304]{0:T(1024)(128)(4,1)S(1)}, s32[]{:S(2)}) async-start(s8[8388608]{0:T(1024)(128)(4,1)} %bitcast.84), calls=%async_computation.6 | async-start | bytes 8388608
  193.8 61.4 %collective-permute-start.1 = (bf16[1024,704]{0,1:T(8,128)(2,1)}, bf16[1024,704]{0,1:T(8,128)(2,1)}, u32[]{:S(2)}, u32[]{:S(2)}) collective-permute-start(bf16[1024,704]{0,1:T(8,128)(2,1)} %fusion.25), channel_id=1, source_target_pairs={{0,1},{1,0},{2,3},{3,2},{4,5},{5,4},{6,7},{7,6},{8,9},{9,8},{10,11... | collective-permute-start | bytes 4325384 | tf_op jit(solution)/shard_map/ppermute | solution.py:326
  195.2 3.4 copy-start.17
  198.0 11.1 %copy-start.15 = (s32[1,16,4]{1,2,0:T(4,128)S(1)}, s32[1,16,4]{1,2,0:T(4,128)}, u32[]{:S(2)}) copy-start(s32[1,16,4]{1,2,0:T(4,128)} %param.16) | copy-start | bytes 772
  198.0 11.4 %copy-start.16 = (s32[1,16]{1,0:T(1,128)S(1)}, s32[1,16]{1,0:T(1,128)}, u32[]{:S(2)}) copy-start(s32[1,16]{1,0:T(1,128)} %param.17) | copy-start | bytes 196
  198.0 87.7 %collective-permute-start = (bf16[1024,704]{0,1:T(8,128)(2,1)}, bf16[1024,704]{0,1:T(8,128)(2,1)}, u32[]{:S(2)}, u32[]{:S(2)}) collective-permute-start(bf16[1024,704]{0,1:T(8,128)(2,1)} %fusion.28), channel_id=1, source_target_pairs={{0,1},{1,0},{2,3},{3,2},{4,5},{5,4},{6,7},{7,6},{8,9},{9,8},{10,11... | collective-permute-start | bytes 4325384 | tf_op jit(solution)/shard_map/ppermute | solution.py:326
  211.0 44.2 %copy-start.14 = (bf16[16,64,2048]{2,1,0:T(8,128)(2,1)S(1)}, bf16[16,64,2048]{2,1,0:T(8,128)(2,1)}, u32[]{:S(2)}) copy-start(bf16[16,64,2048]{2,1,0:T(8,128)(2,1)} %copy-done.12) | copy-start | bytes 12582916
  211.0 44.2 %copy-start.23 = (bf16[1024,704]{0,1:T(8,128)(2,1)S(1)}, bf16[1024,704]{0,1:T(8,128)(2,1)}, u32[]{:S(2)}) copy-start(bf16[1024,704]{0,1:T(8,128)(2,1)} %copy-done.22) | copy-start | bytes 4325380
  229.9 55.8 %copy-start.21 = (bf16[1024,704]{0,1:T(8,128)(2,1)S(1)}, bf16[1024,704]{0,1:T(8,128)(2,1)}, u32[]{:S(2)}) copy-start(bf16[1024,704]{0,1:T(8,128)(2,1)} %copy-done.20) | copy-start | bytes 4325380
  259.8 30.6 %copy-start.6 = (bf16[1,128,1024]{2,1,0:T(8,128)(2,1)S(1)}, bf16[1,128,1024]{2,1,0:T(8,128)(2,1)}, u32[]{:S(2)}) copy-start(bf16[1,128,1024]{2,1,0:T(8,128)(2,1)} %param.13) | copy-start | bytes 786436
  290.4 2.2 copy-start.3
  294.8 35.1 %copy-start.7 = (bf16[1,128,1024]{2,1,0:T(8,128)(2,1)S(1)}, bf16[1,128,1024]{2,1,0:T(8,128)(2,1)}, u32[]{:S(2)}) copy-start(bf16[1,128,1024]{2,1,0:T(8,128)(2,1)} %param.14) | copy-start | bytes 786436
  294.8 35.1 %copy-start.8 = (bf16[1,128,1024]{2,1,0:T(8,128)(2,1)S(1)}, bf16[1,128,1024]{2,1,0:T(8,128)(2,1)}, u32[]{:S(2)}) copy-start(bf16[1,128,1024]{2,1,0:T(8,128)(2,1)} %param.15) | copy-start | bytes 786436
  329.8 16.3 %copy-start.1 = (bf16[1,2048,704]{1,2,0:T(8,128)(2,1)S(1)}, bf16[1,2048,704]{1,2,0:T(8,128)(2,1)}, u32[]{:S(2)}) copy-start(bf16[1,2048,704]{1,2,0:T(8,128)(2,1)} %param.24) | copy-start | bytes 8650756
  329.8 2.3 copy-start.2
  332.2 2.2 copy-start.5
  (3 other events, 5.2 us)
Sparse Core Ops, SparseCore 0:
  10.2 66.9 all-gather.7
  79.3 70.0 all-gather.9
  151.5 54.4 all-gather.11

commit v2 on v1

--- a/solution.py
+++ b/solution.py
@@ -16,10 +16,11 @@
 MESH = pl.DeviceIdType.MESH
 
 
-def ring_gather_kernel(n, x_ref, g_ref, xo_ref, go_ref, ring_send, ring_recv, sib_send, sib_recv, own_sem):
+def ring_gather_kernel(n, count, *refs):
     chips = n // 2
     half_chips = chips // 2
-    rows = x_ref.shape[0]
+    ins, outs = refs[:count], refs[count : 2 * count]
+    ring_send, ring_recv, sib_send, sib_recv, own_sem = refs[2 * count :]
     me = lax.axis_index("ctx")
     core = me % 2
     chip = me // 2
@@ -33,9 +34,9 @@
 
     sibling = me + 1 - 2 * core
     nexts = (device_at(pos + 1), device_at(pos - 1))
-    ins, outs = (x_ref, g_ref), (xo_ref, go_ref)
-
-    def piece(owner, direction, hop):
+
+    def piece(owner, a, direction, hop):
+        rows = ins[a].shape[0]
         if hop < half_chips:
             return pl.ds(pl.multiple_of(owner * rows, rows), rows)
         part = rows // 2
@@ -44,7 +45,7 @@
     def ring_copy(src, owner, a, direction, hop):
         return pltpu.make_async_remote_copy(
             src_ref=src,
-            dst_ref=outs[a].at[piece(owner, direction, hop)],
+            dst_ref=outs[a].at[piece(owner, a, direction, hop)],
             send_sem=ring_send.at[direction, hop - 1, a],
             recv_sem=ring_recv.at[direction, hop - 1, a],
             device_id={"ctx": nexts[direction]},
@@ -68,31 +69,29 @@
 
     sends = []
     sib_waits = []
-    my_rows = pl.ds(pl.multiple_of(me * rows, rows), rows)
-    sib_rows = pl.ds(pl.multiple_of(sibling * rows, rows), rows)
-    for a in (0, 1):
+    for a in range(count):
         for direction in (0, 1):
             c = ring_copy(ins[a], me, a, direction, 1)
             c.start()
             sends.append(c)
     own = []
-    for a in (0, 1):
-        c = sib_copy(ins[a], outs[a].at[my_rows], a, 0)
+    for a in range(count):
+        c = sib_copy(ins[a], outs[a].at[piece(me, a, 0, 1)], a, 0)
         c.start()
         sends.append(c)
-        sib_waits.append(sib_copy(outs[a].at[sib_rows], outs[a].at[sib_rows], a, 0))
-        local = pltpu.make_async_copy(ins[a], outs[a].at[my_rows], own_sem.at[a])
+        sib_waits.append(sib_copy(outs[a].at[piece(sibling, a, 0, 1)], outs[a].at[piece(sibling, a, 0, 1)], a, 0))
+        local = pltpu.make_async_copy(ins[a], outs[a].at[piece(me, a, 0, 1)], own_sem.at[a])
         local.start()
         own.append(local)
     for hop in range(1, half_chips + 1):
-        for a in (0, 1):
+        for a in range(count):
             for direction in (0, 1):
                 step = hop if direction == 0 else -hop
                 owner = device_at(pos - step)
-                here = outs[a].at[piece(owner, direction, hop)]
+                here = outs[a].at[piece(owner, a, direction, hop)]
                 ring_copy(here, owner, a, direction, hop).wait_recv()
                 if hop < half_chips:
-                    onward = outs[a].at[piece(owner, direction, hop + 1)]
+                    onward = outs[a].at[piece(owner, a, direction, hop + 1)]
                     c = ring_copy(onward, owner, a, direction, hop + 1)
                     c.start()
                     sends.append(c)
@@ -101,7 +100,7 @@
                 c.start()
                 sends.append(c)
                 other = owner + 1 - 2 * core
-                there = outs[a].at[piece(other, direction, hop)]
+                there = outs[a].at[piece(other, a, direction, hop)]
                 sib_waits.append(sib_copy(there, there, a, slot))
     for c in own:
         c.wait()
@@ -111,29 +110,33 @@
         c.wait_send()
 
 
-def ring_gather(x, g):
+def ring_gather(arrays, collective_id):
     n = lax.axis_size("ctx")
     hops = n // 4
-    rows, width = x.shape
-    out = jax.ShapeDtypeStruct((n * rows, width), x.dtype)
+    count = len(arrays)
+    anywhere = pl.BlockSpec(memory_space=pl.ANY)
     return pl.pallas_call(
-        functools.partial(ring_gather_kernel, n),
-        out_shape=(out, out),
-        in_specs=[pl.BlockSpec(memory_space=pl.ANY)] * 2,
-        out_specs=(pl.BlockSpec(memory_space=pl.ANY),) * 2,
+        functools.partial(ring_gather_kernel, n, count),
+        out_shape=tuple(
+            jax.ShapeDtypeStruct((n * a.shape[0], a.shape[1]), a.dtype) for a in arrays
+        ),
+        in_specs=[anywhere] * count,
+        out_specs=(anywhere,) * count,
         scratch_shapes=[
-            pltpu.SemaphoreType.DMA((2, hops, 2)),
-            pltpu.SemaphoreType.DMA((2, hops, 2)),
-            pltpu.SemaphoreType.DMA((1 + 2 * hops, 2)),
-            pltpu.SemaphoreType.DMA((1 + 2 * hops, 2)),
-            pltpu.SemaphoreType.DMA((2,)),
+            pltpu.SemaphoreType.DMA((2, hops, count)),
+            pltpu.SemaphoreType.DMA((2, hops, count)),
+            pltpu.SemaphoreType.DMA((1 + 2 * hops, count)),
+            pltpu.SemaphoreType.DMA((1 + 2 * hops, count)),
+            pltpu.SemaphoreType.DMA((count,)),
         ],
-        compiler_params=pltpu.CompilerParams(collective_id=0, has_side_effects=True),
+        compiler_params=pltpu.CompilerParams(collective_id=collective_id, has_side_effects=True),
         cost_estimate=pl.CostEstimate(
-            flops=0, bytes_accessed=4 * n * rows * width * 2, transcendentals=0
-        ),
-        name="ring_gather",
-    )(x, g)
+            flops=0,
+            bytes_accessed=sum(4 * n * a.size * a.dtype.itemsize for a in arrays),
+            transcendentals=0,
+        ),
+        name="ring_gather_%d" % collective_id,
+    )(*arrays)
 
 
 def dot_rows(a, b):
@@ -277,13 +280,8 @@
     experts = jnp.arange(n, dtype=jnp.int32)
     matches = route_experts[0].T[None, :, :] == experts[:, None, None]
     coef_here = jnp.sum(jnp.where(matches, route_weight[0].T[None, :, :], 0.0), axis=1)
-    coef_all = lax.all_gather(coef_here, "ctx", axis=0)
-    coef = lax.dynamic_index_in_dim(coef_all, me, axis=1, keepdims=False)
-
-    k_all = lax.all_gather(key_rows[0], "ctx", axis=0, tiled=True)
-    v_all = lax.all_gather(value_rows[0], "ctx", axis=0, tiled=True)
-    q_all = lax.all_gather(query_rows[0], "ctx", axis=0, tiled=True)
-    x_all, g_all = ring_gather(expert_input[0], layer_grad[0])
+    coef_all, x_all, g_all = ring_gather((coef_here, expert_input[0], layer_grad[0]), 0)
+    coef = lax.dynamic_index_in_dim(coef_all.reshape(n, n, rows), me, axis=1, keepdims=False)
 
     capacity = min(rows, rows * TOPK * 4 // (3 * n))
     present = coef > 0.0
@@ -322,25 +320,17 @@
     if dp == 2:
         half = width // 2
         swap = [(0, 1), (1, 0)]
-        arrived = [
-            lax.ppermute(
-                partial(lax.dynamic_slice_in_dim(a, (1 - my_dp) * half, half, 1), b), "dp", swap
-            )
-            for a, b in pairs
+        leaving = [
+            partial(lax.dynamic_slice_in_dim(a, (1 - my_dp) * half, half, 1), b) for a, b in pairs
         ]
-        sums = [
-            partial(lax.dynamic_slice_in_dim(a, my_dp * half, half, 1), b).astype(jnp.float32)
-            + r.astype(jnp.float32)
-            for (a, b), r in zip(pairs, arrived)
-        ]
+        arrived = [lax.ppermute(a, "dp", swap) for a in leaving]
     else:
-        sums = [
-            lax.psum_scatter(partial(a, b), "dp", scatter_dimension=0, tiled=True).astype(
-                jnp.float32
-            )
-            for a, b in pairs
-        ]
-    down_grad, gate_grad, up_grad = (s[None] for s in sums)
+        leaving = [partial(a, b) for a, b in pairs]
+        arrived = [lax.psum_scatter(a, "dp", scatter_dimension=0, tiled=True) for a in leaving]
+    key_in, value_in, query_in, _ = lax.optimization_barrier(
+        (key_rows[0], value_rows[0], query_rows[0], leaving)
+    )
+    k_all, v_all, q_all = ring_gather((key_in, value_in, query_in), 1)
 
     out_all = lax.dot_general(
         g_all, out_weight, (((1,), (1,)), ((), ())), preferred_element_type=jnp.float32
@@ -374,6 +364,16 @@
         my_open.reshape(BLK, 1),
         offset,
     )
+    if dp == 2:
+        key_grad, right = lax.optimization_barrier((key_grad, [b for _, b in pairs]))
+        sums = [
+            partial(lax.dynamic_slice_in_dim(a, my_dp * half, half, 1), b).astype(jnp.float32)
+            + r.astype(jnp.float32)
+            for (a, _), b, r in zip(pairs, right, arrived)
+        ]
+    else:
+        sums = [r.astype(jnp.float32) for r in arrived]
+    down_grad, gate_grad, up_grad = (s[None] for s in sums)
     return (query_grad[None], key_grad[None], value_grad[None], gate_grad, up_grad, down_grad)
 
 

time: 353 us -> 273 us (0.77)
  waiting for transfers between devices: 66.5 us -> 0.01 us
  Pallas kernels: 154 us -> 181 us
  blocking collectives: 41.1 us -> 19.8 us
  between operations: 14 us -> 0.91 us
  local copies, waits for them, and re-layouts: 15.6 us -> 9.2 us
    ppermute x3, waiting for transfers between devices: 64.4 us -> 0.01 us  [per_device(): arrived = [lax.ppermute(a, 'dp', swap) for a in leaving]]
    pallas_call x1 -> x2, Pallas kernels: 126 us -> 153 us  [ring_gather(): pl.pallas_call(functools.partial(ring_gather_kernel, n, count), out_shape...]
    all_gather x1 -> x0, blocking collectives: 23.7 us -> none  [per_device(): coef_all = lax.all_gather(coef_here, 'ctx', axis=0)]
    unnamed x60 -> x58, local copies, waits for them, and re-layouts: 13.2 us -> 6.53 us
  transfers between devices with their start and end apart: 6 -> 3, of which waited for: 3 -> 0; matrix products, arithmetic and copies ran while one was open for 18% -> 10% of each run, Pallas kernels for 41% -> 34%
where the time goes in v2:
time: 273 us
  Pallas kernels  181 us (66%)
  matrix products  57.4 us (21%)
  blocking collectives  19.8 us (7%)
  local copies, waits for them, and re-layouts  9.2 us (3%)
  starting transfers between devices  3.54 us (1%)
    pallas_call x2, Pallas kernels, ring_gather(): pl.pallas_call(functools.partial(ring_gather_kernel, n, count), out_shape...  153 us
    dot_general x6, matrix products, partial(): lax.dot_general(a, b, (((0,), (0,)), ((), ())), preferred_element_type=jn...  23.2 us
    all_gather x1, blocking collectives, per_device(): stats_all = lax.all_gather(stats, 'ctx', axis=2, tiled=True)  19.8 us
    pallas_call x1, Pallas kernels, query_side(): pl.pallas_call(query_kernel, grid=(heads,), out_shape=(jax.ShapeDtypeStru...  16.7 us
    pallas_call x1, Pallas kernels, key_side(): pl.pallas_call(key_kernel, grid=(heads,), out_shape=(out, out), in_specs=...  11.2 us
    dot_general x1, matrix products, per_device(): lax.dot_general(g_all, out_weight, (((1,), (1,)), ((), ())), preferred_el...  10.5 us
    unnamed x58, local copies, waits for them, and re-layouts  6.53 us
  transfers between devices with their start and end apart: 3, of which 0 were waited for; matrix products, arithmetic and copies ran while one was open for 10% of the time, Pallas kernels for 34%

profile of v2, /device:TPU:0, one launch (start us, length us, event | category | flops | bytes accessed | tf_op | source)
XLA Modules:
  0.0 273.1 jit_solution(8947864720737247676)
XLA Ops:
  0.7 0.8 copy.33
  1.5 0.7 copy.32
  2.2 0.6 select_reduce_fusion.1.refs_0_
  2.8 87.3 %ring_gather_0.1 = (f32[256,128]{1,0:T(8,128)}, bf16[2048,2048]{1,0:T(8,128)(2,1)}, bf16[2048,2048]{1,0:T(8,128)(2,1)}) custom-call(f32[16,128]{1,0:T(8,128)} %select_reduce_fusion.1.refs_0_, bf16[128,2048]{1,0:T(8,128)(2,1)} %bitcast.93, bf16[128,2048]{1,0:T(8,128)(2,1)} %bitcast.94), custom_call_target="tpu_custom_call" | custom-call | bytes 67633152 | tf_op jit(solution)/shard_map/ring_gather_0/pallas_call | solution.py:118
  90.2 0.9 constant_dynamic-slice_fusion.2
  91.0 0.3 reduce_window_sum.14
  91.3 4.8 %convolution_convert_fusion.1 = bf16[16,64,2048]{2,1,0:T(8,128)(2,1)S(1)} fusion(bf16[16,128,2048]{2,1,0:T(8,128)(2,1)} %bitcast.83, s32[16,128]{1,0:T(8,128)S(1)} %broadcast_add_fusion, pred[16,128]{1,0:T(8,128)(4,1)S(1)} %get-tuple-element.43), kind=kOutput, calls=%fused_computation.2 | convolution fusion | flops 539230208 | bytes 12593152 | tf_op jit(solution)/shard_map/ics,isd->icd/dot_general | solution.py:293
  96.1 0.2 select_reduce_fusion
  96.4 4.8 %fusion.2 = f32[1024,704]{0,1:T(8,128)} fusion(bf16[1024,2048]{1,0:T(8,128)(2,1)S(1)} %bitcast.87, bf16[1,2048,704]{1,2,0:T(8,128)(2,1)S(1)} %copy-done.16), kind=kOutput, calls=%fused_computation.5 | convolution fusion | flops 2952790016 | bytes 9961472 | tf_op jit(solution)/shard_map/dot_general | solution.py:304
  101.1 4.8 %fusion.4 = f32[1024,704]{0,1:T(8,128)} fusion(bf16[1024,2048]{1,0:T(8,128)(2,1)S(1)} %bitcast.88, bf16[1,2048,704]{1,2,0:T(8,128)(2,1)S(1)} %copy-done.17), kind=kOutput, calls=%fused_computation.7 | convolution fusion | flops 2952790016 | bytes 9961472 | tf_op jit(solution)/shard_map/dot_general | solution.py:303
  105.9 4.8 %multiply_convert_fusion = bf16[16,64,2048]{2,1,0:T(8,128)(2,1)S(1)} fusion(bf16[16,128,2048]{2,1,0:T(8,128)(2,1)} %bitcast.80, f32[16,64]{1,0:T(8,128)S(1)} %select_reduce_fusion, s32[16,128]{1,0:T(8,128)S(1)} %broadcast_add_fusion, pred[16,128]{1,0:T(8,128)(4,1)S(1)} %get-tuple-element.43), kind=kOutput, calls=%fused_computation | convolution fusion | flops 541327360 | bytes 12597248 | tf_op jit(solution)/shard_map/ics,isd->icd/dot_general | solution.py:296
  110.7 0.2 copy-done.25
  111.0 4.5 %multiply_convert_fusion.1 = (bf16[1024,704]{0,1:T(8,128)(2,1)S(1)}, bf16[1024,704]{0,1:T(8,128)(2,1)S(1)}, bf16[1024,704]{0,1:T(8,128)(2,1)S(1)}) fusion(f32[1024,704]{0,1:T(8,128)S(1)} %copy-done.25, f32[1024,704]{0,1:T(8,128)S(1)} %copy-done.24, bf16[1024,2048]{1,0:T(8,128)(2,1)S(1)} %bitcast.84, bf16[1,2048,704]{1,2,0:T(8,128)(2,1)S(1)} %copy-done), kind=kOutput, calls=%fused_computation.12 | convolution fusion | flops 2963603456 | bytes 17170432 | tf_op jit(solution)/shard_map/dot_general | solution.py:305
  115.5 2.8 %fusion.31 = bf16[1024,704]{0,1:T(8,128)(2,1)} fusion(bf16[1024,704]{0,1:T(8,128)(2,1)S(1)} %get-tuple-element.41, bf16[1024,2048]{1,0:T(8,128)(2,1)S(1)} %bitcast.85, s32[]{:T(128)S(6)} %select_n.32), kind=kOutput, calls=%fused_computation.33 | convolution fusion | flops 1477115904 | bytes 4980740 | tf_op jit(solution)/shard_map/dot_general | solution.py:315
  118.3 1.5 collective-permute-start.2
  119.8 2.8 %fusion.22 = bf16[1024,704]{0,1:T(8,128)(2,1)} fusion(bf16[1024,704]{0,1:T(8,128)(2,1)S(1)} %get-tuple-element.39, bf16[1024,2048]{1,0:T(8,128)(2,1)S(1)} %bitcast.89, s32[]{:T(128)S(6)} %select_n.32), kind=kOutput, calls=%fused_computation.30 | convolution fusion | flops 1477115904 | bytes 4980740 | tf_op jit(solution)/shard_map/dot_general | solution.py:315
  122.6 1.4 collective-permute-start
  124.0 2.8 %fusion.19 = bf16[1024,704]{0,1:T(8,128)(2,1)} fusion(bf16[1024,704]{0,1:T(8,128)(2,1)S(1)} %get-tuple-element.40, bf16[1024,2048]{1,0:T(8,128)(2,1)S(1)} %bitcast.90, s32[]{:T(128)S(6)} %select_n.32), kind=kOutput, calls=%fused_computation.29 | convolution fusion | flops 1477115904 | bytes 4980740 | tf_op jit(solution)/shard_map/dot_general | solution.py:315
  126.8 0.6 collective-permute-start.1
  127.7 0.3 copy-done.15
  128.0 10.5 %convolution_convert_fusion.g_ref = bf16[2048,1024]{1,0:T(8,128)(2,1)} fusion(bf16[2048,2048]{1,0:T(8,128)(2,1)S(1)} %bitcast.82, bf16[1024,2048]{1,0:T(8,128)(2,1)S(1)} %copy-done.15), kind=kOutput, calls=%fused_computation.1 | convolution fusion | flops 8592031744 | bytes 16777216 | tf_op jit(solution)/shard_map/dot_general | solution.py:335
  138.8 0.4 copy.25.open_ref
  139.1 65.7 %ring_gather_1.1 = (bf16[2048,1024]{1,0:T(8,128)(2,1)}, bf16[2048,1024]{1,0:T(8,128)(2,1)}, bf16[2048,1024]{1,0:T(8,128)(2,1)}) custom-call(bf16[128,1024]{1,0:T(8,128)(2,1)} %bitcast.73, bf16[128,1024]{1,0:T(8,128)(2,1)} %bitcast.75, bf16[128,1024]{1,0:T(8,128)(2,1)} %bitcast.71), custom_call_target="tpu_custom_call" | custom-call | bytes 50331648 | tf_op jit(solution)/shard_map/ring_gather_1/pallas_call | solution.py:118
  204.8 1.0 constant_dynamic-slice_fusion.1.g_ref
  205.8 2.2 copy-done.3
  208.0 2.2 copy-done.4
  210.2 16.7 %query_side.1 = (bf16[128,1024]{1,0:T(8,128)(2,1)}, f32[8,1,128]{2,1,0:T(1,128)S(1)}, f32[8,1,128]{2,1,0:T(1,128)S(1)}) custom-call(bf16[128,1024]{1,0:T(8,128)(2,1)S(1)} %bitcast.72, bf16[2048,1024]{1,0:T(8,128)(2,1)S(1)} %copy-done.3, bf16[2048,1024]{1,0:T(8,128)(2,1)S(1)} %copy-done.4, bf16[128,1024]{1,0:T(8,128)(2,1)S(1)} %constant_dynamic-slice_fusion.1.g_ref, ...), custom_call_target="tpu_custom_call" | custom-call | flops 1610612736 | bytes 8388608 | tf_op jit(solution)/shard_map/query_side/pallas_call | solution.py:173
  227.0 19.8 %all_gather.3 = f32[2,8,2048]{2,0,1:T(2,128)S(1)} all-gather(f32[2,8,128]{2,0,1:T(2,128)S(1)} %pad_maximum_fusion), channel_id=1, replica_groups=mesh['ctx'=16,'dp'=2] {'ctx'}, dimensions={2}, use_global_device_ids=true | all-gather | bytes 139264 | tf_op jit(solution)/shard_map/all_gather | solution.py:352
  247.0 11.2 %key_side.1 = (bf16[128,1024]{1,0:T(8,128)(2,1)}, bf16[128,1024]{1,0:T(8,128)(2,1)}) custom-call(bf16[128,1024]{1,0:T(8,128)(2,1)S(1)} %bitcast.74, bf16[128,1024]{1,0:T(8,128)(2,1)S(1)} %bitcast.76, bf16[2048,1024]{1,0:T(8,128)(2,1)S(1)} %copy-done.5, bf16[2048,1024]{1,0:T(8,128)(2,1)S(1)} %copy-done.2, f32[8,1,2048]{2,1,0:T(1,128)S(1)} %get-tuple-element.48.lt_ref, ...), custom_call_target="tpu_custom_call" | custom-call | flops 2147483648 | bytes 8388608 | tf_op jit(solution)/shard_map/key_side/pallas_call | solution.py:230
  258.2 5.4 %add_bitcast_fusion = f32[1,1024,704]{1,2,0:T(8,128)} fusion(bf16[1024,704]{0,1:T(8,128)(2,1)} %collective-permute-done.2, bf16[1024,704]{0,1:T(8,128)(2,1)S(1)} %copy-done.23, bf16[1024,2048]{1,0:T(8,128)(2,1)} %bitcast.86, s32[]{:T(128)S(6)} %select_n.34), kind=kOutput, calls=%fused_computation.9 | convolution fusion | flops 1479278592 | bytes 7864324 | tf_op jit(solution)/shard_map/dot_general | solution.py:315
  263.6 4.7 %add_bitcast_fusion.2 = f32[1,1024,704]{1,2,0:T(8,128)} fusion(bf16[1024,704]{0,1:T(8,128)(2,1)} %collective-permute-done, bf16[1024,704]{0,1:T(8,128)(2,1)S(1)} %copy-done.21, bf16[1024,2048]{1,0:T(8,128)(2,1)S(1)} %bitcast.91, s32[]{:T(128)S(6)} %select_n.34), kind=kOutput, calls=%fused_computation.11 | convolution fusion | flops 1479278592 | bytes 7864324 | tf_op jit(solution)/shard_map/dot_general | solution.py:315
  268.3 4.8 %add_bitcast_fusion.1 = f32[1,1024,704]{1,2,0:T(8,128)} fusion(bf16[1024,704]{0,1:T(8,128)(2,1)} %collective-permute-done.1, bf16[1024,704]{0,1:T(8,128)(2,1)S(1)} %copy-done.19, bf16[1024,2048]{1,0:T(8,128)(2,1)S(1)} %bitcast.92, s32[]{:T(128)S(6)} %select_n.34), kind=kOutput, calls=%fused_computation.10 | convolution fusion | flops 1479278592 | bytes 7864324 | tf_op jit(solution)/shard_map/dot_general | solution.py:315
  (68 shorter events, 0.8 us)
Async XLA Ops:
  0.6 110.1 %copy-start = (bf16[1,2048,704]{1,2,0:T(8,128)(2,1)S(1)}, bf16[1,2048,704]{1,2,0:T(8,128)(2,1)}, u32[]{:S(2)}) copy-start(bf16[1,2048,704]{1,2,0:T(8,128)(2,1)} %param.25) | copy-start | bytes 8650756
  91.3 5.0 %copy-start.16 = (bf16[1,2048,704]{1,2,0:T(8,128)(2,1)S(1)}, bf16[1,2048,704]{1,2,0:T(8,128)(2,1)}, u32[]{:S(2)}) copy-start(bf16[1,2048,704]{1,2,0:T(8,128)(2,1)} %param.24) | copy-start | bytes 8650756
  96.1 5.0 %copy-start.10 = (bf16[16,64,2048]{2,1,0:T(8,128)(2,1)}, bf16[16,64,2048]{2,1,0:T(8,128)(2,1)S(1)}, u32[]{:S(2)}) copy-start(bf16[16,64,2048]{2,1,0:T(8,128)(2,1)S(1)} %convolution_convert_fusion.1) | copy-start | bytes 12582916
  96.4 4.8 %copy-start.17 = (bf16[1,2048,704]{1,2,0:T(8,128)(2,1)S(1)}, bf16[1,2048,704]{1,2,0:T(8,128)(2,1)}, u32[]{:S(2)}) copy-start(bf16[1,2048,704]{1,2,0:T(8,128)(2,1)} %param.23) | copy-start | bytes 8650756
  105.9 4.8 %copy-start.24 = (f32[1024,704]{0,1:T(8,128)S(1)}, f32[1024,704]{0,1:T(8,128)}, u32[]{:S(2)}) copy-start(f32[1024,704]{0,1:T(8,128)} %fusion.2) | copy-start | bytes 8650756
  105.9 5.1 %copy-start.25 = (f32[1024,704]{0,1:T(8,128)S(1)}, f32[1024,704]{0,1:T(8,128)}, u32[]{:S(2)}) copy-start(f32[1024,704]{0,1:T(8,128)} %fusion.4) | copy-start | bytes 8650756
  110.7 4.8 %copy-start.9 = (bf16[16,64,2048]{2,1,0:T(8,128)(2,1)}, bf16[16,64,2048]{2,1,0:T(8,128)(2,1)S(1)}, u32[]{:S(2)}) copy-start(bf16[16,64,2048]{2,1,0:T(8,128)(2,1)S(1)} %multiply_convert_fusion) | copy-start | bytes 12582916
  115.5 2.8 %copy-start.22 = (bf16[1024,704]{0,1:T(8,128)(2,1)}, bf16[1024,704]{0,1:T(8,128)(2,1)S(1)}, u32[]{:S(2)}) copy-start(bf16[1024,704]{0,1:T(8,128)(2,1)S(1)} %get-tuple-element.41) | copy-start | bytes 4325380
  115.5 4.3 %copy-start.20 = (bf16[1024,704]{0,1:T(8,128)(2,1)}, bf16[1024,704]{0,1:T(8,128)(2,1)S(1)}, u32[]{:S(2)}) copy-start(bf16[1024,704]{0,1:T(8,128)(2,1)S(1)} %get-tuple-element.39) | copy-start | bytes 4325380
  115.5 8.5 %copy-start.18 = (bf16[1024,704]{0,1:T(8,128)(2,1)}, bf16[1024,704]{0,1:T(8,128)(2,1)S(1)}, u32[]{:S(2)}) copy-start(bf16[1024,704]{0,1:T(8,128)(2,1)S(1)} %get-tuple-element.40) | copy-start | bytes 4325380
  115.5 4.3 %copy-start.11 = (bf16[16,64,2048]{2,1,0:T(8,128)(2,1)S(1)}, bf16[16,64,2048]{2,1,0:T(8,128)(2,1)}, u32[]{:S(2)}) copy-start(bf16[16,64,2048]{2,1,0:T(8,128)(2,1)} %copy-done.10) | copy-start | bytes 12582916
  118.3 139.9 %collective-permute-start.2 = (bf16[1024,704]{0,1:T(8,128)(2,1)}, bf16[1024,704]{0,1:T(8,128)(2,1)}, u32[]{:S(2)}, u32[]{:S(2)}) collective-permute-start(bf16[1024,704]{0,1:T(8,128)(2,1)} %fusion.31), channel_id=1, source_target_pairs={{0,1},{1,0},{2,3},{3,2},{4,5},{5,4},{6,7},{7,6},{8,9},{9,8},{10,11... | collective-permute-start | bytes 4325384 | tf_op jit(solution)/shard_map/ppermute | solution.py:326
  119.8 7.9 %slice-start = ((s8[8388608]{0:T(1024)(128)(4,1)}), s8[4194304]{0:T(1024)(128)(4,1)S(1)}, s32[]{:S(2)}) async-start(s8[8388608]{0:T(1024)(128)(4,1)} %bitcast.81), calls=%async_computation | async-start | bytes 8388608
  122.6 141.0 %collective-permute-start = (bf16[1024,704]{0,1:T(8,128)(2,1)}, bf16[1024,704]{0,1:T(8,128)(2,1)}, u32[]{:S(2)}, u32[]{:S(2)}) collective-permute-start(bf16[1024,704]{0,1:T(8,128)(2,1)} %fusion.22), channel_id=1, source_target_pairs={{0,1},{1,0},{2,3},{3,2},{4,5},{5,4},{6,7},{7,6},{8,9},{9,8},{10,11... | collective-permute-start | bytes 4325384 | tf_op jit(solution)/shard_map/ppermute | solution.py:326
  124.0 3.4 %copy-start.13 = (s32[1,16,4]{1,2,0:T(4,128)S(1)}, s32[1,16,4]{1,2,0:T(4,128)}, u32[]{:S(2)}) copy-start(s32[1,16,4]{1,2,0:T(4,128)} %param.16) | copy-start | bytes 772
  124.0 3.7 %slice-start.1 = ((s8[8388608]{0:T(1024)(128)(4,1)}), s8[4194304]{0:T(1024)(128)(4,1)S(1)}, s32[]{:S(2)}) async-start(s8[8388608]{0:T(1024)(128)(4,1)} %bitcast.81), calls=%async_computation.1 | async-start | bytes 8388608
  124.0 4.0 %copy-start.15 = (bf16[1024,2048]{1,0:T(8,128)(2,1)S(1)}, bf16[1024,2048]{1,0:T(8,128)(2,1)}, u32[]{:S(2)}) copy-start(bf16[1024,2048]{1,0:T(8,128)(2,1)} %param.18) | copy-start | bytes 12582916
  126.8 141.5 %collective-permute-start.1 = (bf16[1024,704]{0,1:T(8,128)(2,1)}, bf16[1024,704]{0,1:T(8,128)(2,1)}, u32[]{:S(2)}, u32[]{:S(2)}) collective-permute-start(bf16[1024,704]{0,1:T(8,128)(2,1)} %fusion.19), channel_id=1, source_target_pairs={{0,1},{1,0},{2,3},{3,2},{4,5},{5,4},{6,7},{7,6},{8,9},{9,8},{10,11... | collective-permute-start | bytes 4325384 | tf_op jit(solution)/shard_map/ppermute | solution.py:326
  128.0 10.6 %copy-start.14 = (s32[1,16]{1,0:T(1,128)S(1)}, s32[1,16]{1,0:T(1,128)}, u32[]{:S(2)}) copy-start(s32[1,16]{1,0:T(1,128)} %param.17) | copy-start | bytes 196
  128.0 77.9 %copy-start.6 = (bf16[1,128,1024]{2,1,0:T(8,128)(2,1)S(1)}, bf16[1,128,1024]{2,1,0:T(8,128)(2,1)}, u32[]{:S(2)}) copy-start(bf16[1,128,1024]{2,1,0:T(8,128)(2,1)} %param.13) | copy-start | bytes 786436
  205.8 2.2 copy-start.3
  208.0 2.2 copy-start.4
  210.2 36.7 %copy-start.2 = (bf16[2048,1024]{1,0:T(8,128)(2,1)S(1)}, bf16[2048,1024]{1,0:T(8,128)(2,1)}, u32[]{:S(2)}) copy-start(bf16[2048,1024]{1,0:T(8,128)(2,1)} %convolution_convert_fusion.g_ref) | copy-start | bytes 12582916
  210.2 36.7 %copy-start.5 = (bf16[2048,1024]{1,0:T(8,128)(2,1)S(1)}, bf16[2048,1024]{1,0:T(8,128)(2,1)}, u32[]{:S(2)}) copy-start(bf16[2048,1024]{1,0:T(8,128)(2,1)} %get-tuple-element.33.q_ref) | copy-start | bytes 12582916
  210.2 36.8 %copy-start.7 = (bf16[1,128,1024]{2,1,0:T(8,128)(2,1)S(1)}, bf16[1,128,1024]{2,1,0:T(8,128)(2,1)}, u32[]{:S(2)}) copy-start(bf16[1,128,1024]{2,1,0:T(8,128)(2,1)} %param.14) | copy-start | bytes 786436
  210.2 36.8 %copy-start.8 = (bf16[1,128,1024]{2,1,0:T(8,128)(2,1)S(1)}, bf16[1,128,1024]{2,1,0:T(8,128)(2,1)}, u32[]{:S(2)}) copy-start(bf16[1,128,1024]{2,1,0:T(8,128)(2,1)} %param.15) | copy-start | bytes 786436
  247.0 11.2 %copy-start.23 = (bf16[1024,704]{0,1:T(8,128)(2,1)S(1)}, bf16[1024,704]{0,1:T(8,128)(2,1)}, u32[]{:S(2)}) copy-start(bf16[1024,704]{0,1:T(8,128)(2,1)} %copy-done.22) | copy-start | bytes 4325380
  258.2 5.4 %copy-start.12 = (bf16[16,64,2048]{2,1,0:T(8,128)(2,1)S(1)}, bf16[16,64,2048]{2,1,0:T(8,128)(2,1)}, u32[]{:S(2)}) copy-start(bf16[16,64,2048]{2,1,0:T(8,128)(2,1)} %copy-done.10) | copy-start | bytes 12582916
  258.2 5.4 %copy-start.21 = (bf16[1024,704]{0,1:T(8,128)(2,1)S(1)}, bf16[1024,704]{0,1:T(8,128)(2,1)}, u32[]{:S(2)}) copy-start(bf16[1024,704]{0,1:T(8,128)(2,1)} %copy-done.20) | copy-start | bytes 4325380
  263.6 4.8 %copy-start.19 = (bf16[1024,704]{0,1:T(8,128)(2,1)S(1)}, bf16[1024,704]{0,1:T(8,128)(2,1)}, u32[]{:S(2)}) copy-start(bf16[1024,704]{0,1:T(8,128)(2,1)} %copy-done.18) | copy-start | bytes 4325380
  268.3 4.8 %copy-start.1 = (bf16[1,2048,704]{1,2,0:T(8,128)(2,1)S(1)}, bf16[1,2048,704]{1,2,0:T(8,128)(2,1)}, u32[]{:S(2)}) copy-start(bf16[1,2048,704]{1,2,0:T(8,128)(2,1)} %param.25) | copy-start | bytes 8650756

commit v3 on v2

--- a/solution.py
+++ b/solution.py
@@ -281,6 +281,8 @@
     matches = route_experts[0].T[None, :, :] == experts[:, None, None]
     coef_here = jnp.sum(jnp.where(matches, route_weight[0].T[None, :, :], 0.0), axis=1)
     coef_all, x_all, g_all = ring_gather((coef_here, expert_input[0], layer_grad[0]), 0)
+    query_in, coef_all = lax.optimization_barrier((query_rows[0], coef_all))
+    q_all = lax.all_gather(query_in, "ctx", axis=0, tiled=True)
     coef = lax.dynamic_index_in_dim(coef_all.reshape(n, n, rows), me, axis=1, keepdims=False)
 
     capacity = min(rows, rows * TOPK * 4 // (3 * n))
@@ -327,10 +329,8 @@
     else:
         leaving = [partial(a, b) for a, b in pairs]
         arrived = [lax.psum_scatter(a, "dp", scatter_dimension=0, tiled=True) for a in leaving]
-    key_in, value_in, query_in, _ = lax.optimization_barrier(
-        (key_rows[0], value_rows[0], query_rows[0], leaving)
-    )
-    k_all, v_all, q_all = ring_gather((key_in, value_in, query_in), 1)
+    key_in, value_in, _ = lax.optimization_barrier((key_rows[0], value_rows[0], leaving))
+    k_all, v_all = ring_gather((key_in, value_in), 1)
 
     out_all = lax.dot_general(
         g_all, out_weight, (((1,), (1,)), ((), ())), preferred_element_type=jnp.float32

time: 273 us -> 269 us (0.985)
  Pallas kernels: 181 us -> 160 us
  between operations: 0.91 us -> 14.3 us
  local copies, waits for them, and re-layouts: 9.2 us -> 13 us
    pallas_call x2, Pallas kernels: 153 us -> 133 us  [ring_gather(): pl.pallas_call(functools.partial(ring_gather_kernel, n, count), out_shape...]
    unnamed x58 -> x56, local copies, waits for them, and re-layouts: 6.53 us -> 10.4 us
  transfers between devices with their start and end apart: 3 -> 4, of which waited for: 0 -> 0; matrix products, arithmetic and copies ran while one was open for 10% -> 21% of each run, Pallas kernels for 34% -> 27%
where the time goes in v3:
time: 269 us
  Pallas kernels  160 us (59%)
  matrix products  56.8 us (21%)
  blocking collectives  19.8 us (7%)
  between operations  14.3 us (5%)
  local copies, waits for them, and re-layouts  13 us (5%)
  starting transfers between devices  3.54 us (1%)
    pallas_call x2, Pallas kernels, ring_gather(): pl.pallas_call(functools.partial(ring_gather_kernel, n, count), out_shape...  133 us
    dot_general x6, matrix products, partial(): lax.dot_general(a, b, (((0,), (0,)), ((), ())), preferred_element_type=jn...  22.6 us
    all_gather x1, blocking collectives, per_device(): stats_all = lax.all_gather(stats, 'ctx', axis=2, tiled=True)  19.8 us
    pallas_call x1, Pallas kernels, query_side(): pl.pallas_call(query_kernel, grid=(heads,), out_shape=(jax.ShapeDtypeStru...  16.7 us
    pallas_call x1, Pallas kernels, key_side(): pl.pallas_call(key_kernel, grid=(heads,), out_shape=(out, out), in_specs=...  10.9 us
    dot_general x1, matrix products, per_device(): lax.dot_general(g_all, out_weight, (((1,), (1,)), ((), ())), preferred_el...  10.7 us
    unnamed x56, local copies, waits for them, and re-layouts  10.4 us
    dot_general x1, matrix products, per_device(): jnp.einsum('ics,isd->icd', onehot, g_all.reshape(n, rows, width), preferr...  6.83 us
  transfers between devices with their start and end apart: 4, of which 0 were waited for; matrix products, arithmetic and copies ran while one was open for 21% of the time, Pallas kernels for 27%

profile of v3, /device:TPU:0, one launch (start us, length us, event | category | flops | bytes accessed | tf_op | source)
XLA Modules:
  0.0 269.1 jit_solution(17468474462814846719)
XLA Ops:
  7.2 0.8 copy.33
  8.1 0.7 copy.32
  8.8 0.6 select_reduce_fusion.1.refs_0_
  9.4 87.3 %ring_gather_0.1 = (f32[256,128]{1,0:T(8,128)}, bf16[2048,2048]{1,0:T(8,128)(2,1)}, bf16[2048,2048]{1,0:T(8,128)(2,1)}) custom-call(f32[16,128]{1,0:T(8,128)} %select_reduce_fusion.1.refs_0_, bf16[128,2048]{1,0:T(8,128)(2,1)} %bitcast.95, bf16[128,2048]{1,0:T(8,128)(2,1)} %bitcast.96), custom_call_target="tpu_custom_call" | custom-call | bytes 67633152 | tf_op jit(solution)/shard_map/ring_gather_0/pallas_call | solution.py:118
  96.7 0.9 constant_dynamic-slice_fusion.2
  97.6 0.3 reduce_window_sum.14
  97.9 0.2 select_reduce_fusion
  98.1 6.8 %multiply_convert_fusion = bf16[16,64,2048]{2,1,0:T(8,128)(2,1)} fusion(bf16[16,128,2048]{2,1,0:T(8,128)(2,1)} %bitcast.80, f32[16,64]{1,0:T(8,128)S(1)} %select_reduce_fusion, s32[16,128]{1,0:T(8,128)S(1)} %broadcast_add_fusion, pred[16,128]{1,0:T(8,128)(4,1)S(1)} %get-tuple-element.43), kind=kOutput, calls=%fused_computation | convolution fusion | flops 541327360 | bytes 12597248 | tf_op jit(solution)/shard_map/ics,isd->icd/dot_general | solution.py:298
  105.0 3.2 %convolution_convert_fusion.1 = bf16[16,64,2048]{2,1,0:T(8,128)(2,1)} fusion(bf16[16,128,2048]{2,1,0:T(8,128)(2,1)S(1)} %bitcast.85, s32[16,128]{1,0:T(8,128)S(1)} %broadcast_add_fusion, pred[16,128]{1,0:T(8,128)(4,1)S(1)} %get-tuple-element.43), kind=kOutput, calls=%fused_computation.2 | convolution fusion | flops 539230208 | bytes 12593152 | tf_op jit(solution)/shard_map/ics,isd->icd/dot_general | solution.py:295
  108.2 6.0 %fusion.2 = f32[1024,704]{0,1:T(8,128)S(1)} fusion(bf16[1024,2048]{1,0:T(8,128)(2,1)} %bitcast.89, bf16[1,2048,704]{1,2,0:T(8,128)(2,1)} %param.24), kind=kOutput, calls=%fused_computation.5 | convolution fusion | flops 2952790016 | bytes 9961472 | tf_op jit(solution)/shard_map/dot_general | solution.py:306
  114.3 3.2 %fusion.4 = f32[1024,704]{0,1:T(8,128)S(1)} fusion(bf16[1024,2048]{1,0:T(8,128)(2,1)S(1)} %bitcast.90, bf16[1,2048,704]{1,2,0:T(8,128)(2,1)S(1)} %copy-done.16), kind=kOutput, calls=%fused_computation.7 | convolution fusion | flops 2952790016 | bytes 9961472 | tf_op jit(solution)/shard_map/dot_general | solution.py:305
  117.5 4.2 %multiply_convert_fusion.1 = (bf16[1024,704]{0,1:T(8,128)(2,1)S(1)}, bf16[1024,704]{0,1:T(8,128)(2,1)S(1)}, bf16[1024,704]{0,1:T(8,128)(2,1)S(1)}) fusion(f32[1024,704]{0,1:T(8,128)S(1)} %fusion.4, f32[1024,704]{0,1:T(8,128)S(1)} %fusion.2, bf16[1024,2048]{1,0:T(8,128)(2,1)S(1)} %bitcast.86, bf16[1,2048,704]{1,2,0:T(8,128)(2,1)S(1)} %copy-done), kind=kOutput, calls=%fused_computation.12 | convolution fusion | flops 2963603456 | bytes 17170432 | tf_op jit(solution)/shard_map/dot_general | solution.py:307
  121.7 2.8 %fusion.31 = bf16[1024,704]{0,1:T(8,128)(2,1)} fusion(bf16[1024,704]{0,1:T(8,128)(2,1)S(1)} %get-tuple-element.41, bf16[1024,2048]{1,0:T(8,128)(2,1)S(1)} %bitcast.87, s32[]{:T(128)S(6)} %select_n.32), kind=kOutput, calls=%fused_computation.33 | convolution fusion | flops 1477115904 | bytes 4980740 | tf_op jit(solution)/shard_map/dot_general | solution.py:317
  124.5 1.5 collective-permute-start.2
  126.0 2.8 %fusion.22 = bf16[1024,704]{0,1:T(8,128)(2,1)} fusion(bf16[1024,704]{0,1:T(8,128)(2,1)S(1)} %get-tuple-element.39, bf16[1024,2048]{1,0:T(8,128)(2,1)S(1)} %bitcast.91, s32[]{:T(128)S(6)} %select_n.32), kind=kOutput, calls=%fused_computation.30 | convolution fusion | flops 1477115904 | bytes 4980740 | tf_op jit(solution)/shard_map/dot_general | solution.py:317
  128.8 0.6 collective-permute-start
  129.3 2.8 %fusion.19 = bf16[1024,704]{0,1:T(8,128)(2,1)} fusion(bf16[1024,704]{0,1:T(8,128)(2,1)S(1)} %get-tuple-element.40, bf16[1024,2048]{1,0:T(8,128)(2,1)S(1)} %bitcast.92, s32[]{:T(128)S(6)} %select_n.32), kind=kOutput, calls=%fused_computation.29 | convolution fusion | flops 1477115904 | bytes 4980740 | tf_op jit(solution)/shard_map/dot_general | solution.py:317
  132.1 1.5 collective-permute-start.1
  133.9 10.7 %convolution_convert_fusion.g_ref = bf16[2048,1024]{1,0:T(8,128)(2,1)} fusion(bf16[2048,2048]{1,0:T(8,128)(2,1)S(1)} %bitcast.82, bf16[1024,2048]{1,0:T(8,128)(2,1)S(1)} %copy-done.15), kind=kOutput, calls=%fused_computation.1 | convolution fusion | flops 8592031744 | bytes 16777216 | tf_op jit(solution)/shard_map/dot_general | solution.py:335
  144.9 0.4 copy.25.open_ref
  145.2 45.2 %ring_gather_1.1 = (bf16[2048,1024]{1,0:T(8,128)(2,1)}, bf16[2048,1024]{1,0:T(8,128)(2,1)}) custom-call(bf16[128,1024]{1,0:T(8,128)(2,1)} %bitcast.73, bf16[128,1024]{1,0:T(8,128)(2,1)} %bitcast.75), custom_call_target="tpu_custom_call" | custom-call | bytes 33554432 | tf_op jit(solution)/shard_map/ring_gather_1/pallas_call | solution.py:118
  190.4 1.0 constant_dynamic-slice_fusion.1.g_ref
  191.4 2.2 copy-done.3
  193.6 2.2 copy-done.4
  195.8 16.7 %query_side.1 = (bf16[128,1024]{1,0:T(8,128)(2,1)}, f32[8,1,128]{2,1,0:T(1,128)S(1)}, f32[8,1,128]{2,1,0:T(1,128)S(1)}) custom-call(bf16[128,1024]{1,0:T(8,128)(2,1)S(1)} %bitcast.72, bf16[2048,1024]{1,0:T(8,128)(2,1)S(1)} %copy-done.3, bf16[2048,1024]{1,0:T(8,128)(2,1)S(1)} %copy-done.4, bf16[128,1024]{1,0:T(8,128)(2,1)S(1)} %constant_dynamic-slice_fusion.1.g_ref, ...), custom_call_target="tpu_custom_call" | custom-call | flops 1610612736 | bytes 8388608 | tf_op jit(solution)/shard_map/query_side/pallas_call | solution.py:173
  212.6 19.8 %all_gather.7 = f32[2,8,2048]{2,0,1:T(2,128)S(1)} all-gather(f32[2,8,128]{2,0,1:T(2,128)S(1)} %pad_maximum_fusion), channel_id=1, replica_groups=mesh['ctx'=16,'dp'=2] {'ctx'}, dimensions={2}, use_global_device_ids=true | all-gather | bytes 139264 | tf_op jit(solution)/shard_map/all_gather | solution.py:352
  232.6 2.2 copy-done.2
  234.8 2.2 copy-done.5
  237.0 10.9 %key_side.1 = (bf16[128,1024]{1,0:T(8,128)(2,1)}, bf16[128,1024]{1,0:T(8,128)(2,1)}) custom-call(bf16[128,1024]{1,0:T(8,128)(2,1)S(1)} %bitcast.74, bf16[128,1024]{1,0:T(8,128)(2,1)S(1)} %bitcast.76, bf16[2048,1024]{1,0:T(8,128)(2,1)S(1)} %copy-done.5, bf16[2048,1024]{1,0:T(8,128)(2,1)S(1)} %copy-done.2, f32[8,1,2048]{2,1,0:T(1,128)S(1)} %get-tuple-element.48.lt_ref, ...), custom_call_target="tpu_custom_call" | custom-call | flops 2147483648 | bytes 8388608 | tf_op jit(solution)/shard_map/key_side/pallas_call | solution.py:230
  247.9 4.8 %add_bitcast_fusion = f32[1,1024,704]{1,2,0:T(8,128)} fusion(bf16[1024,704]{0,1:T(8,128)(2,1)} %collective-permute-done.2, bf16[1024,704]{0,1:T(8,128)(2,1)S(1)} %copy-done.22, bf16[1024,2048]{1,0:T(8,128)(2,1)S(1)} %bitcast.88, s32[]{:T(128)S(6)} %select_n.34), kind=kOutput, calls=%fused_computation.9 | convolution fusion | flops 1479278592 | bytes 7864324 | tf_op jit(solution)/shard_map/dot_general | solution.py:317
  252.7 4.7 %add_bitcast_fusion.2 = f32[1,1024,704]{1,2,0:T(8,128)} fusion(bf16[1024,704]{0,1:T(8,128)(2,1)} %collective-permute-done, bf16[1024,704]{0,1:T(8,128)(2,1)S(1)} %copy-done.20, bf16[1024,2048]{1,0:T(8,128)(2,1)S(1)} %bitcast.93, s32[]{:T(128)S(6)} %select_n.34), kind=kOutput, calls=%fused_computation.11 | convolution fusion | flops 1479278592 | bytes 7864324 | tf_op jit(solution)/shard_map/dot_general | solution.py:317
  257.4 4.8 %add_bitcast_fusion.1 = f32[1,1024,704]{1,2,0:T(8,128)} fusion(bf16[1024,704]{0,1:T(8,128)(2,1)} %collective-permute-done.1, bf16[1024,704]{0,1:T(8,128)(2,1)S(1)} %copy-done.18, bf16[1024,2048]{1,0:T(8,128)(2,1)S(1)} %bitcast.94, s32[]{:T(128)S(6)} %select_n.34), kind=kOutput, calls=%fused_computation.10 | convolution fusion | flops 1479278592 | bytes 7864324 | tf_op jit(solution)/shard_map/dot_general | solution.py:317
  (70 shorter events, 0.9 us)
Async XLA Ops:
  7.2 110.3 %copy-start = (bf16[1,2048,704]{1,2,0:T(8,128)(2,1)S(1)}, bf16[1,2048,704]{1,2,0:T(8,128)(2,1)}, u32[]{:S(2)}) copy-start(bf16[1,2048,704]{1,2,0:T(8,128)(2,1)} %param.25) | copy-start | bytes 8650756
  7.2 225.3 %all-gather.2.cloned.1.call-start = ((), (), s32[]{:S(2)}) async-start(), calls=%async_computation | async-start | bytes 4456448 | tf_op jit(solution)/shard_map/all_gather | solution.py:285
  98.1 6.9 %slice-start.2 = ((s8[8388608]{0:T(1024)(128)(4,1)}), s8[4194304]{0:T(1024)(128)(4,1)S(1)}, s32[]{:S(2)}) async-start(s8[8388608]{0:T(1024)(128)(4,1)} %bitcast.83), calls=%async_computation.3 | async-start | bytes 8388608
  98.1 6.8 %slice-start.3 = ((s8[8388608]{0:T(1024)(128)(4,1)}), s8[4194304]{0:T(1024)(128)(4,1)S(1)}, s32[]{:S(2)}) async-start(s8[8388608]{0:T(1024)(128)(4,1)} %bitcast.83), calls=%async_computation.4 | async-start | bytes 8388608
  108.2 6.0 %copy-start.11 = (bf16[16,64,2048]{2,1,0:T(8,128)(2,1)S(1)}, bf16[16,64,2048]{2,1,0:T(8,128)(2,1)}, u32[]{:S(2)}) copy-start(bf16[16,64,2048]{2,1,0:T(8,128)(2,1)} %convolution_convert_fusion.1) | copy-start | bytes 12582916
  108.2 6.0 %copy-start.16 = (bf16[1,2048,704]{1,2,0:T(8,128)(2,1)S(1)}, bf16[1,2048,704]{1,2,0:T(8,128)(2,1)}, u32[]{:S(2)}) copy-start(bf16[1,2048,704]{1,2,0:T(8,128)(2,1)} %param.23) | copy-start | bytes 8650756
  114.3 3.2 %copy-start.9 = (bf16[16,64,2048]{2,1,0:T(8,128)(2,1)S(1)}, bf16[16,64,2048]{2,1,0:T(8,128)(2,1)}, u32[]{:S(2)}) copy-start(bf16[16,64,2048]{2,1,0:T(8,128)(2,1)} %multiply_convert_fusion) | copy-start | bytes 12582916
  121.7 2.8 %copy-start.21 = (bf16[1024,704]{0,1:T(8,128)(2,1)}, bf16[1024,704]{0,1:T(8,128)(2,1)S(1)}, u32[]{:S(2)}) copy-start(bf16[1024,704]{0,1:T(8,128)(2,1)S(1)} %get-tuple-element.41) | copy-start | bytes 4325380
  121.7 4.3 %copy-start.19 = (bf16[1024,704]{0,1:T(8,128)(2,1)}, bf16[1024,704]{0,1:T(8,128)(2,1)S(1)}, u32[]{:S(2)}) copy-start(bf16[1024,704]{0,1:T(8,128)(2,1)S(1)} %get-tuple-element.39) | copy-start | bytes 4325380
  121.7 7.6 %copy-start.17 = (bf16[1024,704]{0,1:T(8,128)(2,1)}, bf16[1024,704]{0,1:T(8,128)(2,1)S(1)}, u32[]{:S(2)}) copy-start(bf16[1024,704]{0,1:T(8,128)(2,1)S(1)} %get-tuple-element.40) | copy-start | bytes 4325380
  124.5 123.4 %collective-permute-start.2 = (bf16[1024,704]{0,1:T(8,128)(2,1)}, bf16[1024,704]{0,1:T(8,128)(2,1)}, u32[]{:S(2)}, u32[]{:S(2)}) collective-permute-start(bf16[1024,704]{0,1:T(8,128)(2,1)} %fusion.31), channel_id=1, source_target_pairs={{0,1},{1,0},{2,3},{3,2},{4,5},{5,4},{6,7},{7,6},{8,9},{9,8},{10,11... | collective-permute-start | bytes 4325384 | tf_op jit(solution)/shard_map/ppermute | solution.py:328
  126.0 7.9 %slice-start = ((s8[8388608]{0:T(1024)(128)(4,1)}), s8[4194304]{0:T(1024)(128)(4,1)S(1)}, s32[]{:S(2)}) async-start(s8[8388608]{0:T(1024)(128)(4,1)} %bitcast.81), calls=%async_computation.1 | async-start | bytes 8388608
  128.8 123.9 %collective-permute-start = (bf16[1024,704]{0,1:T(8,128)(2,1)}, bf16[1024,704]{0,1:T(8,128)(2,1)}, u32[]{:S(2)}, u32[]{:S(2)}) collective-permute-start(bf16[1024,704]{0,1:T(8,128)(2,1)} %fusion.22), channel_id=1, source_target_pairs={{0,1},{1,0},{2,3},{3,2},{4,5},{5,4},{6,7},{7,6},{8,9},{9,8},{10,11... | collective-permute-start | bytes 4325384 | tf_op jit(solution)/shard_map/ppermute | solution.py:328
  129.3 4.3 %copy-start.13 = (s32[1,16,4]{1,2,0:T(4,128)S(1)}, s32[1,16,4]{1,2,0:T(4,128)}, u32[]{:S(2)}) copy-start(s32[1,16,4]{1,2,0:T(4,128)} %param.16) | copy-start | bytes 772
  129.3 4.5 %slice-start.1 = ((s8[8388608]{0:T(1024)(128)(4,1)}), s8[4194304]{0:T(1024)(128)(4,1)S(1)}, s32[]{:S(2)}) async-start(s8[8388608]{0:T(1024)(128)(4,1)} %bitcast.81), calls=%async_computation.2 | async-start | bytes 8388608
  129.3 4.5 %copy-start.15 = (bf16[1024,2048]{1,0:T(8,128)(2,1)S(1)}, bf16[1024,2048]{1,0:T(8,128)(2,1)}, u32[]{:S(2)}) copy-start(bf16[1024,2048]{1,0:T(8,128)(2,1)} %param.18) | copy-start | bytes 12582916
  132.1 125.3 %collective-permute-start.1 = (bf16[1024,704]{0,1:T(8,128)(2,1)}, bf16[1024,704]{0,1:T(8,128)(2,1)}, u32[]{:S(2)}, u32[]{:S(2)}) collective-permute-start(bf16[1024,704]{0,1:T(8,128)(2,1)} %fusion.19), channel_id=1, source_target_pairs={{0,1},{1,0},{2,3},{3,2},{4,5},{5,4},{6,7},{7,6},{8,9},{9,8},{10,11... | collective-permute-start | bytes 4325384 | tf_op jit(solution)/shard_map/ppermute | solution.py:328
  133.9 10.8 %copy-start.14 = (s32[1,16]{1,0:T(1,128)S(1)}, s32[1,16]{1,0:T(1,128)}, u32[]{:S(2)}) copy-start(s32[1,16]{1,0:T(1,128)} %param.17) | copy-start | bytes 196
  133.9 57.5 %copy-start.6 = (bf16[1,128,1024]{2,1,0:T(8,128)(2,1)S(1)}, bf16[1,128,1024]{2,1,0:T(8,128)(2,1)}, u32[]{:S(2)}) copy-start(bf16[1,128,1024]{2,1,0:T(8,128)(2,1)} %param.13) | copy-start | bytes 786436
  191.4 2.2 copy-start.3
  193.6 2.2 copy-start.4
  195.8 36.8 %copy-start.7 = (bf16[1,128,1024]{2,1,0:T(8,128)(2,1)S(1)}, bf16[1,128,1024]{2,1,0:T(8,128)(2,1)}, u32[]{:S(2)}) copy-start(bf16[1,128,1024]{2,1,0:T(8,128)(2,1)} %param.14) | copy-start | bytes 786436
  195.8 36.8 %copy-start.8 = (bf16[1,128,1024]{2,1,0:T(8,128)(2,1)S(1)}, bf16[1,128,1024]{2,1,0:T(8,128)(2,1)}, u32[]{:S(2)}) copy-start(bf16[1,128,1024]{2,1,0:T(8,128)(2,1)} %param.15) | copy-start | bytes 786436
  232.6 2.2 copy-start.2
  234.8 2.2 copy-start.5
  237.0 10.9 %copy-start.10 = (bf16[16,64,2048]{2,1,0:T(8,128)(2,1)S(1)}, bf16[16,64,2048]{2,1,0:T(8,128)(2,1)}, u32[]{:S(2)}) copy-start(bf16[16,64,2048]{2,1,0:T(8,128)(2,1)} %multiply_convert_fusion) | copy-start | bytes 12582916
  237.0 10.9 %copy-start.22 = (bf16[1024,704]{0,1:T(8,128)(2,1)S(1)}, bf16[1024,704]{0,1:T(8,128)(2,1)}, u32[]{:S(2)}) copy-start(bf16[1024,704]{0,1:T(8,128)(2,1)} %copy-done.21) | copy-start | bytes 4325380
  247.9 4.8 %copy-start.12 = (bf16[16,64,2048]{2,1,0:T(8,128)(2,1)S(1)}, bf16[16,64,2048]{2,1,0:T(8,128)(2,1)}, u32[]{:S(2)}) copy-start(bf16[16,64,2048]{2,1,0:T(8,128)(2,1)} %convolution_convert_fusion.1) | copy-start | bytes 12582916
  247.9 4.8 %copy-start.20 = (bf16[1024,704]{0,1:T(8,128)(2,1)S(1)}, bf16[1024,704]{0,1:T(8,128)(2,1)}, u32[]{:S(2)}) copy-start(bf16[1024,704]{0,1:T(8,128)(2,1)} %copy-done.19) | copy-start | bytes 4325380
  252.7 4.8 %copy-start.18 = (bf16[1024,704]{0,1:T(8,128)(2,1)S(1)}, bf16[1024,704]{0,1:T(8,128)(2,1)}, u32[]{:S(2)}) copy-start(bf16[1024,704]{0,1:T(8,128)(2,1)} %copy-done.17) | copy-start | bytes 4325380
  257.4 4.8 %copy-start.1 = (bf16[1,2048,704]{1,2,0:T(8,128)(2,1)S(1)}, bf16[1,2048,704]{1,2,0:T(8,128)(2,1)}, u32[]{:S(2)}) copy-start(bf16[1,2048,704]{1,2,0:T(8,128)(2,1)} %param.25) | copy-start | bytes 8650756
Sparse Core Ops, SparseCore 0:
  96.9 50.8 all-gather.1
